TPU v7x, 128 devices: a whole 4x4x4 slice. The times are simulated.
128 devices in a mesh: mode: 16 (over z_lo, x, core), mesh: 8 (over z_hi, y).
Axes of the slice: x: 4, y: 4, z: 4 (z_hi: 2, z_lo: 2; z = z_hi * 2 + z_lo), core: 2. Of those that a mesh axis runs over, the one named last changes fastest.
Arguments:
- velocity: float32 [3, 11, 11, 8, 32, 512], P(None, None, None, 'mesh', 'mode'), may hold values from -6 to 6
- penalty: float32 [11, 11, 8, 32], P(None, None, 'mesh'), may hold values from 0.5 to 8
Outputs:
- solution: float32 [512, 3, 11, 11, 8, 32], P('mode', None, None, None, 'mesh')
All inputs are finite; a program needn't handle non-finite values.
Results may differ from a plain program's by a relative error of at most 0.0001.
Values sent between devices are 32-bit elements; how exact they have to be, the bound alone decides.
A program may use at most 256 MiB of HBM per device.

v0:
```python
import math

import jax
import jax.numpy as jnp
import numpy as np
from jax import lax
from jax.sharding import PartitionSpec as P

ORDER = 10
PLANES = 512
MODES = 256
ITERS = 6


helm_base = 1.0
span_wave = 0.02
bound_ratio = 25.0


def shifted(array, axis, by):
    devices = lax.axis_size(axis)
    pairs = [(i, i + by) for i in range(devices) if 0 <= i + by < devices]
    return lax.ppermute(array, axis, pairs)


def legendre_pair(points, order):
    previous = points * 0.0 + 1.0
    current = points * 1.0
    for degree in range(2, order + 1):
        following = ((2 * degree - 1) * points * current - (degree - 1) * previous) / degree
        previous = current
        current = following
    return (current, previous)


def gll_tables(order):
    count = order + 1
    points = -np.cos(np.pi * np.arange(count) / order)
    for sweep in range(200):
        top_vals, below_vals = legendre_pair(points, order)
        points = points - (points * top_vals - below_vals) / (count * top_vals)
    legendre_vals, below_vals = legendre_pair(points, order)
    weights = 2.0 / (order * (order + 1) * legendre_vals**2)
    identity = np.eye(count)
    spacing = points[:, None] - points[None, :] + identity
    derivative = legendre_vals[:, None] / (legendre_vals[None, :] * spacing) * (1.0 - identity)
    corner = np.concatenate(
        [[-order * (order + 1) / 4.0], np.zeros(order - 1), [order * (order + 1) / 4.0]]
    )
    derivative = derivative + identity * corner[None, :]
    stiffness = derivative.T @ (weights[:, None] * derivative)
    weight_mat = identity * weights[None, :]
    laplace = np.kron(stiffness, weight_mat) + np.kron(weight_mat, stiffness)
    upper_bound = float(
        np.max(np.sum(np.abs(laplace), axis=1) / np.sum(laplace * np.eye(count * count), axis=1))
    )
    weight_vec = jnp.asarray(weights, jnp.float32)
    stiff_mat = jnp.asarray(stiffness, jnp.float32)
    deriv_mat = jnp.asarray(derivative, jnp.float32)
    mass_two = weight_vec[:, None] * weight_vec[None, :]
    stiff_diag = jnp.diagonal(stiff_mat)
    lap_diag = stiff_diag[:, None] * weight_vec[None, :] + weight_vec[:, None] * stiff_diag[None, :]
    return (weight_vec, stiff_mat, deriv_mat, mass_two, lap_diag, upper_bound)


def dft_table(planes, modes):
    plane_index = jnp.arange(planes, dtype=jnp.int32)
    mode_index = jnp.arange(modes, dtype=jnp.int32)
    phase_turns = plane_index[:, None] * mode_index[None, :] % planes
    angles = 2.0 * math.pi / planes * phase_turns.astype(jnp.float32)
    return jnp.concatenate([jnp.cos(angles), -jnp.sin(angles)], axis=1) / math.sqrt(planes)


def advect(along_first, along_second, field, deriv_mat):
    grad_first = jnp.einsum(
        "ia,...abxyz->...ibxyz", deriv_mat, field, precision=lax.Precision.HIGHEST
    )
    grad_second = jnp.einsum(
        "jb,...abxyz->...ajxyz", deriv_mat, field, precision=lax.Precision.HIGHEST
    )
    return field - (along_first * grad_first + along_second * grad_second)


def make_coeff(first_row, count, penalty, mass_two):
    rows = (first_row + jnp.arange(count, dtype=jnp.int32)).astype(jnp.int32)
    wave = (rows % MODES).astype(jnp.float32)
    helm = helm_base + (span_wave * wave) ** 2
    return (helm[:, None, None, None, None, None] + penalty[None, None]) * mass_two[
        None, None, :, :, None, None
    ]


def assemble(field, neighbours):
    top = field[:, :, :, -1]
    bottom = field[:, :, :, 0]
    shared = top[..., :-1] + bottom[..., 1:]
    top_new = jnp.concatenate([shared, top[..., -1:]], axis=-1)
    bottom_new = jnp.concatenate([bottom[..., :1], shared], axis=-1)
    field = field.at[:, :, :, -1].set(top_new).at[:, :, :, 0].set(bottom_new)
    right = field[:, :, -1]
    left = field[:, :, 0]
    shared = right[:, :, :, :-1] + left[:, :, :, 1:]
    from_lower, from_upper = neighbours(right[:, :, :, -1], left[:, :, :, 0])
    right_new = jnp.concatenate([shared, (right[:, :, :, -1] + from_upper)[:, :, :, None]], axis=3)
    left_new = jnp.concatenate([(left[:, :, :, 0] + from_lower)[:, :, :, None], shared], axis=3)
    return field.at[:, :, -1].set(right_new).at[:, :, 0].set(left_new)


def strip_neighbours(right_edge, left_edge):
    from_lower = shifted(right_edge, "mesh", 1)
    from_upper = shifted(left_edge, "mesh", -1)
    return (from_lower, from_upper)


def helm_apply(field, coeff, stiff_mat, weight_vec):
    along_first = jnp.einsum("ia,rcabxy->rcibxy", stiff_mat, field, precision=lax.Precision.HIGHEST)
    along_second = jnp.einsum(
        "jb,rcabxy->rcajxy", stiff_mat, field, precision=lax.Precision.HIGHEST
    )
    along_first = along_first * weight_vec[None, None, None, :, None, None]
    along_second = along_second * weight_vec[None, None, :, None, None, None]
    return along_first + along_second + coeff * field


def chebyshev(spectra, coeff, tables, neighbours):
    weight_vec, stiff_mat, deriv_mat, mass_two, lap_diag, upper_bound = tables
    lower_bound = upper_bound / bound_ratio
    midpoint = (upper_bound + lower_bound) / 2.0
    half_width = (upper_bound - lower_bound) / 2.0
    rhs = assemble(mass_two[None, None, :, :, None, None] * spectra, neighbours)
    diagonal = assemble(lap_diag[None, None, :, :, None, None] + coeff, neighbours)
    inverse = 1.0 / diagonal
    iterate = jnp.zeros_like(rhs)
    residual = rhs
    direction = inverse * residual / midpoint
    recurrence = half_width / midpoint
    for step in range(ITERS):
        iterate = iterate + direction
        residual = residual - assemble(
            helm_apply(direction, coeff, stiff_mat, weight_vec), neighbours
        )
        if step + 1 < ITERS:
            recurrence_next = 1.0 / (2.0 * midpoint / half_width - recurrence)
            direction = (
                recurrence_next * recurrence * direction
                + 2.0 * recurrence_next / half_width * inverse * residual
            )
            recurrence = recurrence_next
    return iterate


def per_device(velocity, penalty):
    tables = gll_tables(ORDER)
    forcing = advect(velocity[0], velocity[1], velocity, tables[2])
    table = dft_table(PLANES, MODES)
    spectra = jnp.einsum("cabxyz,zk->kcabxy", forcing, table, precision=lax.Precision.HIGHEST)
    owned = lax.all_to_all(spectra, "mode", split_axis=0, concat_axis=5, tiled=True)
    row_count = owned.shape[0]
    first_row = lax.axis_index("mode") * row_count
    coeff = make_coeff(first_row, row_count, penalty, tables[3])
    return chebyshev(owned, coeff, tables, strip_neighbours)


def solution(mesh):
    return jax.shard_map(
        per_device,
        mesh=mesh,
        in_specs=(P(None, None, None, "mesh", "mode", None), P(None, None, "mesh", None)),
        out_specs=P("mode", None, None, None, "mesh", None),
        check_vma=False,
    )
```

profile of v0, /device:TPU:24, one launch (start us, length us, event | category | flops | bytes accessed | tf_op | source)
XLA Modules:
  0.0 782.0 jit_solution(17833868281497278231)
XLA Ops:
  3.8 3.4 fusion.22
  10.2 4.1 fusion.26
  14.4 18.9 %copy.398 = f32[512,3,11,11,1,2]{3,5,2,1,4,0:T(2,128)} copy(f32[512,3,11,11,1,2]{0,3,5,2,1,4:T(8,128)S(1)} %fusion.26) | data formatting | bytes 2973696 | tf_op jit(solution)/shard_map/cabxyz,zk->kcabxy/dot_general | solution.py:156
  33.2 27.0 %reshape.1472 = f32[16,1,23232]{2,1,0:T(1,128)} reshape(f32[512,1,3,11,2,11]{5,4,3,2,1,0:T(2,128)} %bitcast.386) | data formatting | bytes 2973696
  60.3 5.8 all-to-all-start
  74.1 6.8 collective-permute-start.1
  83.0 3.2 collective-permute-done.1
  90.1 6.2 scatter.99
  96.9 6.6 reduce.56
  103.5 36.3 %reshape.1473 = f32[512,1,3,11,2,11]{5,4,3,2,1,0:T(2,128)} reshape(f32[16,23232]{1,0:T(8,128)} %reduce.56) | data formatting | bytes 2973696
  139.8 24.9 %copy.467 = f32[16,32,3,11,11,1,2]{1,0,6,4,3,2,5:T(8,128)} copy(f32[16,32,3,11,11,1,2]{4,6,3,2,1,0,5:T(2,128)} %bitcast.387) | data formatting | bytes 2973696 | tf_op jit(solution)/shard_map/all_to_all | solution.py:157
  164.8 8.3 %copy.400 = f32[32,3,11,11,1,16,2]{0,6,5,3,2,1,4:T(2,128)} copy(f32[32,3,11,11,1,16,2]{0,5,6,3,2,1,4:T(8,128)} %bitcast.390) | data formatting | bytes 2973696 | tf_op jit(solution)/shard_map/all_to_all | solution.py:157
  173.1 10.4 %copy.401 = f32[32,3,11,11,1,32]{5,2,3,1,0,4:T(8,128)} copy(f32[32,3,11,11,1,32]{0,5,3,2,1,4:T(8,128)} %bitcast.391) | data formatting | bytes 2973696 | tf_op jit(solution)/shard_map/all_to_all | solution.py:157
  183.5 4.1 broadcast_multiply_fusion
  188.8 3.4 copy-done.1
  195.0 6.7 multiply_bitcast_fusion.1
  201.7 7.5 collective-permute-start.3
  212.4 7.2 collective-permute-done.3
  221.2 15.2 %scatter.104 = f32[32,3,11,11,1,32]{5,2,3,1,0,4:T(8,128)} dynamic-update-slice(f32[32,3,11,11,1,32]{5,2,3,1,0,4:T(8,128)} %copy-done.1, f32[32,3,1,11,1,32]{5,2,3,1,0,4:T(1,128)S(1)} %copy.409, s32[]{:T(128)} %constant.647.clone.1, s32[]{:T(128)} %constant.647.clone.1, s32[]{:T(128)} %constant.651.clone.1, s32[]{:T(128)} %constant.647.clone.1, s32[]{:T(128)} %constant.647.clone.1, s32[]{:T(128)} %constant.647.clone.1) | dynamic-update-slice | bytes 270340 | tf_op jit(solution)/shard_map/scatter | solution.py:106
  236.4 14.8 %scatter.105 = f32[32,3,11,11,1,32]{5,2,3,1,0,4:T(8,128)} dynamic-update-slice(f32[32,3,11,11,1,32]{5,2,3,1,0,4:T(8,128)} %scatter.104, f32[32,3,1,11,1,32]{5,2,3,1,0,4:T(1,128)} %copy.410, s32[]{:T(128)} %constant.647.clone.1, s32[]{:T(128)} %constant.647.clone.1, s32[]{:T(128)} %constant.647.clone.1, s32[]{:T(128)} %constant.647.clone.1, s32[]{:T(128)} %constant.647.clone.1, s32[]{:T(128)} %constant.647.clone.1) | dynamic-update-slice | bytes 270340 | tf_op jit(solution)/shard_map/scatter | solution.py:106
  251.2 5.2 multiply_bitcast_fusion
  256.4 11.6 %fusion.14 = f32[32,3,11,32,11]{3,4,2,1,0:T(8,128)} fusion(f32[11,11,1,1,1]{1,0,4,3,2:T(8,128)S(1)} %copy-done.12, f32[32,3,11,11,32]{4,2,3,1,0:T(8,128)S(1)} %multiply_bitcast_fusion), kind=kOutput, calls=%fused_computation.30 | convolution fusion | flops 49065984 | bytes 2974180 | tf_op jit(solution)/shard_map/jb,rcabxy->rcajxy/dot_general | solution.py:117
  268.0 25.3 %fusion.5 = f32[32,3,11,11,1,32]{5,2,3,1,0,4:T(8,128)} fusion(f32[32,3,11,32,11]{3,4,2,1,0:T(8,128)} %fusion.14, f32[32,3,11,11,1,32]{5,2,3,1,0,4:T(8,128)} %scatter.105, f32[11]{0:T(128)S(1)} %copy-done.14, f32[32,11,11,32]{3,1,2,0:T(8,128)} %get-tuple-element.386, f32[32,11,11,32]{3,1,2,0:T(8,128)} %get-tuple-element.378, ...), kind=kOutput, calls=%fused_computation.19 | convolution fusion | flops 52039680 | bytes 5452304 | tf_op jit(solution)/shard_map/ia,rcabxy->rcibxy/dot_general | solution.py:116
  297.8 4.3 fusion.72
  304.9 8.0 %collective-permute-start.5 = (f32[32,3,11,32]{3,0,2,1:T(8,128)}, f32[32,3,11,32]{3,0,2,1:T(8,128)}, u32[]{:S(2)}, u32[]{:S(2)}) collective-permute-start(f32[32,3,11,32]{3,0,2,1:T(8,128)} %bitcast.371), channel_id=1, source_target_pairs={{0,1},{1,2},{2,3},{3,4},{4,5},{5,6},{6,7},{8,9},{9,10},{10,11},{11... | collective-permute-start | bytes 405512 | tf_op jit(solution)/shard_map/ppermute | solution.py:23
  312.9 7.5 collective-permute-done.4
  321.9 15.0 %scatter.110 = f32[32,3,11,11,1,32]{5,2,3,1,0,4:T(8,128)} dynamic-update-slice(f32[32,3,11,11,1,32]{5,2,3,1,0,4:T(8,128)} %fusion.38, f32[32,3,1,11,1,32]{5,2,3,1,0,4:T(1,128)} %copy.420, s32[]{:T(128)} %constant.647.clone.1, s32[]{:T(128)} %constant.647.clone.1, s32[]{:T(128)} %constant.651.clone.1, s32[]{:T(128)} %constant.647.clone.1, s32[]{:T(128)} %constant.647.clone.1, s32[]{:T(128)} %constant.647.clone.1) | dynamic-update-slice | bytes 270340 | tf_op jit(solution)/shard_map/scatter | solution.py:106
  338.7 14.9 %scatter.111 = f32[32,3,11,11,1,32]{5,2,3,1,0,4:T(8,128)} dynamic-update-slice(f32[32,3,11,11,1,32]{5,2,3,1,0,4:T(8,128)} %scatter.110, f32[32,3,1,11,1,32]{5,2,3,1,0,4:T(1,128)S(1)} %copy.421, s32[]{:T(128)} %constant.647.clone.1, s32[]{:T(128)} %constant.647.clone.1, s32[]{:T(128)} %constant.647.clone.1, s32[]{:T(128)} %constant.647.clone.1, s32[]{:T(128)} %constant.647.clone.1, s32[]{:T(128)} %constant.647.clone.1) | dynamic-update-slice | bytes 270340 | tf_op jit(solution)/shard_map/scatter | solution.py:106
  353.5 12.0 %multiply_add_fusion.3 = (f32[32,3,11,11,1,32]{5,2,3,1,0,4:T(8,128)S(1)}, f32[32,3,11,11,1,32]{5,2,3,1,0,4:T(8,128)}) fusion(f32[32,3,11,11,1,32]{5,2,3,1,0,4:T(8,128)} %scatter.105, f32[32,11,11,32]{3,1,2,0:T(8,128)} %get-tuple-element.374, f32[32,11,11,32]{3,1,2,0:T(8,128)} %get-tuple-element.378, f32[32,3,11,11,1,32]{5,2,3,1,0,4:T(8,128)} %scatter.111), kind=kLoop, calls=%fused_computation.36 | loop fusion | flops 1858560 | bytes 6938624 | tf_op jit(solution)/shard_map/add | solution.py:145
  365.6 11.7 %fusion.12 = f32[32,3,11,32,11]{3,4,2,1,0:T(8,128)} fusion(f32[11,11,1,1,1]{1,0,4,3,2:T(8,128)S(1)} %copy-done.12, f32[32,3,11,11,32]{4,2,3,1,0:T(8,128)S(1)} %bitcast.384), kind=kOutput, calls=%fused_computation.28 | convolution fusion | flops 49065984 | bytes 2974180 | tf_op jit(solution)/shard_map/jb,rcabxy->rcajxy/dot_general | solution.py:117
  377.3 14.1 %fusion.4 = f32[32,3,11,11,1,32]{5,2,3,1,0,4:T(8,128)} fusion(f32[32,3,11,32,11]{3,4,2,1,0:T(8,128)} %fusion.12, f32[32,3,11,11,1,32]{5,2,3,1,0,4:T(8,128)S(1)} %get-tuple-element.347, f32[11]{0:T(128)S(1)} %copy-done.14, f32[32,11,11,32]{3,1,2,0:T(8,128)S(1)} %get-tuple-element.385, f32[11,11,1,1,1]{1,0,4,3,2:T(8,128)S(1)} %copy-done.12), kind=kOutput, calls=%fused_computation.15 | convolution fusion | flops 50924544 | bytes 4956688 | tf_op jit(solution)/shard_map/ia,rcabxy->rcibxy/dot_general | solution.py:116
  395.8 4.3 fusion.71
  402.2 7.5 collective-permute-start.7
  409.7 7.4 collective-permute-done.6
  417.7 15.3 %scatter.116 = f32[32,3,11,11,1,32]{5,2,3,1,0,4:T(8,128)} dynamic-update-slice(f32[32,3,11,11,1,32]{5,2,3,1,0,4:T(8,128)} %fusion.40, f32[32,3,1,11,1,32]{5,2,3,1,0,4:T(1,128)S(1)} %copy.430, s32[]{:T(128)} %constant.647.clone.1, s32[]{:T(128)} %constant.647.clone.1, s32[]{:T(128)} %constant.651.clone.1, s32[]{:T(128)} %constant.647.clone.1, s32[]{:T(128)} %constant.647.clone.1, s32[]{:T(128)} %constant.647.clone.1) | dynamic-update-slice | bytes 270340 | tf_op jit(solution)/shard_map/scatter | solution.py:106
  433.6 14.8 %scatter.119 = f32[32,3,11,11,1,32]{5,2,3,1,0,4:T(8,128)} dynamic-update-slice(f32[32,3,11,11,1,32]{5,2,3,1,0,4:T(8,128)} %scatter.116, f32[32,3,1,11,1,32]{5,2,3,1,0,4:T(1,128)S(1)} %copy.431, s32[]{:T(128)} %constant.647.clone.1, s32[]{:T(128)} %constant.647.clone.1, s32[]{:T(128)} %constant.647.clone.1, s32[]{:T(128)} %constant.647.clone.1, s32[]{:T(128)} %constant.647.clone.1, s32[]{:T(128)} %constant.647.clone.1) | dynamic-update-slice | bytes 270340 | tf_op jit(solution)/shard_map/scatter | solution.py:106
  448.4 13.8 %multiply_add_fusion.2 = (f32[32,3,11,11,1,32]{5,2,3,1,0,4:T(8,128)S(1)}, f32[32,3,11,11,1,32]{5,2,3,1,0,4:T(8,128)}) fusion(f32[32,3,11,11,1,32]{5,2,3,1,0,4:T(8,128)} %copy-done.2, f32[32,11,11,32]{3,1,2,0:T(8,128)} %get-tuple-element.375, f32[32,3,11,11,1,32]{5,2,3,1,0,4:T(8,128)} %get-tuple-element.348, f32[32,3,11,11,1,32]{5,2,3,1,0,4:T(8,128)} %scatter.119), kind=kLoop, calls=%fused_computation.35 | loop fusion | flops 1486848 | bytes 7929856 | tf_op jit(solution)/shard_map/add | solution.py:145
  462.3 11.8 %fusion.10 = f32[32,3,11,32,11]{3,4,2,1,0:T(8,128)} fusion(f32[11,11,1,1,1]{1,0,4,3,2:T(8,128)S(1)} %copy-done.12, f32[32,3,11,11,32]{4,2,3,1,0:T(8,128)S(1)} %bitcast.385), kind=kOutput, calls=%fused_computation.26 | convolution fusion | flops 49065984 | bytes 2974180 | tf_op jit(solution)/shard_map/jb,rcabxy->rcajxy/dot_general | solution.py:117
  474.1 14.9 %fusion.3 = f32[32,3,11,11,1,32]{5,2,3,1,0,4:T(8,128)} fusion(f32[32,3,11,32,11]{3,4,2,1,0:T(8,128)} %fusion.10, f32[32,3,11,11,1,32]{5,2,3,1,0,4:T(8,128)S(1)} %get-tuple-element.345, f32[11]{0:T(128)S(1)} %copy-done.14, f32[32,11,11,32]{3,1,2,0:T(8,128)S(1)} %copy-done.5, f32[11,11,1,1,1]{1,0,4,3,2:T(8,128)S(1)} %copy-done.12), kind=kOutput, calls=%fused_computation.11 | convolution fusion | flops 50924544 | bytes 4956688 | tf_op jit(solution)/shard_map/ia,rcabxy->rcibxy/dot_general | solution.py:116
  493.4 4.3 fusion.70
  499.8 7.5 collective-permute-start.9
  507.3 6.4 collective-permute-done.8
  514.4 14.8 %scatter.124 = f32[32,3,11,11,1,32]{5,2,3,1,0,4:T(8,128)} dynamic-update-slice(f32[32,3,11,11,1,32]{5,2,3,1,0,4:T(8,128)} %fusion.42, f32[32,3,1,11,1,32]{5,2,3,1,0,4:T(1,128)S(1)} %copy.440, s32[]{:T(128)} %constant.647.clone.1, s32[]{:T(128)} %constant.647.clone.1, s32[]{:T(128)} %constant.651.clone.1, s32[]{:T(128)} %constant.647.clone.1, s32[]{:T(128)} %constant.647.clone.1, s32[]{:T(128)} %constant.647.clone.1) | dynamic-update-slice | bytes 270340 | tf_op jit(solution)/shard_map/scatter | solution.py:106
  529.9 14.8 %scatter.125 = f32[32,3,11,11,1,32]{5,2,3,1,0,4:T(8,128)} dynamic-update-slice(f32[32,3,11,11,1,32]{5,2,3,1,0,4:T(8,128)} %scatter.124, f32[32,3,1,11,1,32]{5,2,3,1,0,4:T(1,128)S(1)} %copy.441, s32[]{:T(128)} %constant.647.clone.1, s32[]{:T(128)} %constant.647.clone.1, s32[]{:T(128)} %constant.647.clone.1, s32[]{:T(128)} %constant.647.clone.1, s32[]{:T(128)} %constant.647.clone.1, s32[]{:T(128)} %constant.647.clone.1) | dynamic-update-slice | bytes 270340 | tf_op jit(solution)/shard_map/scatter | solution.py:106
  544.7 13.8 %multiply_add_fusion.1 = (f32[32,3,11,11,1,32]{5,2,3,1,0,4:T(8,128)S(1)}, f32[32,3,11,11,1,32]{5,2,3,1,0,4:T(8,128)}) fusion(f32[32,3,11,11,1,32]{5,2,3,1,0,4:T(8,128)} %copy-done.3, f32[32,11,11,32]{3,1,2,0:T(8,128)} %get-tuple-element.376, f32[32,3,11,11,1,32]{5,2,3,1,0,4:T(8,128)} %get-tuple-element.346, f32[32,3,11,11,1,32]{5,2,3,1,0,4:T(8,128)} %scatter.125), kind=kLoop, calls=%fused_computation.34 | loop fusion | flops 1486848 | bytes 7929856 | tf_op jit(solution)/shard_map/add | solution.py:145
  558.5 11.7 %fusion.8 = f32[32,3,11,32,11]{3,4,2,1,0:T(8,128)} fusion(f32[11,11,1,1,1]{1,0,4,3,2:T(8,128)S(1)} %copy-done.12, f32[32,3,11,11,32]{4,2,3,1,0:T(8,128)S(1)} %bitcast.383), kind=kOutput, calls=%fused_computation.24 | convolution fusion | flops 49065984 | bytes 2974180 | tf_op jit(solution)/shard_map/jb,rcabxy->rcajxy/dot_general | solution.py:117
  570.2 15.0 %fusion.2 = f32[32,3,11,11,1,32]{5,2,3,1,0,4:T(8,128)} fusion(f32[32,3,11,32,11]{3,4,2,1,0:T(8,128)} %fusion.8, f32[32,3,11,11,1,32]{5,2,3,1,0,4:T(8,128)S(1)} %get-tuple-element.343, f32[11]{0:T(128)S(1)} %copy-done.14, f32[32,11,11,32]{3,1,2,0:T(8,128)S(1)} %copy-done.6, f32[11,11,1,1,1]{1,0,4,3,2:T(8,128)S(1)} %copy-done.12), kind=kOutput, calls=%fused_computation.7 | convolution fusion | flops 50924544 | bytes 4956688 | tf_op jit(solution)/shard_map/ia,rcabxy->rcibxy/dot_general | solution.py:116
  589.7 4.3 fusion.69
  596.0 7.5 collective-permute-start.11
  603.6 5.5 collective-permute-done.10
  609.8 14.8 %scatter.130 = f32[32,3,11,11,1,32]{5,2,3,1,0,4:T(8,128)} dynamic-update-slice(f32[32,3,11,11,1,32]{5,2,3,1,0,4:T(8,128)} %fusion.44, f32[32,3,1,11,1,32]{5,2,3,1,0,4:T(1,128)S(1)} %copy.450, s32[]{:T(128)} %constant.647.clone.1, s32[]{:T(128)} %constant.647.clone.1, s32[]{:T(128)} %constant.651.clone.1, s32[]{:T(128)} %constant.647.clone.1, s32[]{:T(128)} %constant.647.clone.1, s32[]{:T(128)} %constant.647.clone.1) | dynamic-update-slice | bytes 270340 | tf_op jit(solution)/shard_map/scatter | solution.py:106
  625.2 14.8 %scatter.131 = f32[32,3,11,11,1,32]{5,2,3,1,0,4:T(8,128)} dynamic-update-slice(f32[32,3,11,11,1,32]{5,2,3,1,0,4:T(8,128)} %scatter.130, f32[32,3,1,11,1,32]{5,2,3,1,0,4:T(1,128)S(1)} %copy.451, s32[]{:T(128)} %constant.647.clone.1, s32[]{:T(128)} %constant.647.clone.1, s32[]{:T(128)} %constant.647.clone.1, s32[]{:T(128)} %constant.647.clone.1, s32[]{:T(128)} %constant.647.clone.1, s32[]{:T(128)} %constant.647.clone.1) | dynamic-update-slice | bytes 270340 | tf_op jit(solution)/shard_map/scatter | solution.py:106
  640.0 13.8 %fusion.16 = (f32[32,3,11,11,32]{4,2,3,1,0:T(8,128)S(1)}, f32[32,3,11,11,1,32]{5,2,3,1,0,4:T(8,128)}) fusion(f32[32,11,11,32]{3,1,2,0:T(8,128)} %get-tuple-element.377, f32[32,3,11,11,1,32]{5,2,3,1,0,4:T(8,128)} %copy-done, f32[32,3,11,11,1,32]{5,2,3,1,0,4:T(8,128)} %get-tuple-element.344, f32[32,3,11,11,1,32]{5,2,3,1,0,4:T(8,128)} %scatter.131), kind=kLoop, calls=%fused_computation.45 | loop fusion | flops 1486848 | bytes 7929856 | tf_op jit(solution)/shard_map/reshape.1210
  653.8 12.1 %fusion.6 = f32[32,3,11,32,11]{3,4,2,1,0:T(8,128)} fusion(f32[11,11,1,1,1]{1,0,4,3,2:T(8,128)S(1)} %copy-done.12, f32[32,3,11,11,32]{4,2,3,1,0:T(8,128)S(1)} %get-tuple-element.341), kind=kOutput, calls=%fused_computation.22 | convolution fusion | flops 49065984 | bytes 2974180 | tf_op jit(solution)/shard_map/jb,rcabxy->rcajxy/dot_general | solution.py:117
  666.0 8.5 %fusion.74 = f32[32,3,11,32,11]{3,4,2,1,0:T(8,128)S(1)} fusion(f32[32,3,11,11,32]{4,2,3,1,0:T(8,128)S(1)} %get-tuple-element.341, f32[11,11,1,1,1]{1,0,4,3,2:T(8,128)S(1)} %copy-done.12), kind=kOutput, calls=%fused_computation.181 | convolution fusion | flops 49065984 | bytes 2974180 | tf_op jit(solution)/shard_map/ia,rcabxy->rcibxy/dot_general | solution.py:116
  674.5 6.4 fusion.1
  680.9 18.4 %fusion = f32[32,3,11,11,1,32]{5,2,3,1,0,4:T(8,128)} fusion(f32[32,3,11,11,1,32]{5,3,2,1,0,4:T(8,128)} %fusion.1, f32[32,3,11,32,11]{3,4,2,1,0:T(8,128)} %fusion.6, f32[32,11,11,32]{3,1,2,0:T(8,128)S(1)} %copy-done.7, f32[11]{0:T(128)S(1)} %copy-done.14, f32[32,3,11,11,1,32]{5,2,3,1,0,4:T(8,128)} %get-tuple-element.342, ...), kind=kLoop, calls=%fused_computation.2 | loop fusion | flops 2601984 | bytes 8425516 | tf_op jit(solution)/shard_map/add | solution.py:122
  703.7 4.3 fusion.68
  710.9 7.5 collective-permute-start.13
  718.4 4.5 collective-permute-done.12
  724.4 14.8 %scatter.136 = f32[32,3,11,11,1,32]{5,2,3,1,0,4:T(8,128)} dynamic-update-slice(f32[32,3,11,11,1,32]{5,2,3,1,0,4:T(8,128)} %fusion.46, f32[32,3,1,11,1,32]{5,2,3,1,0,4:T(1,128)} %copy.461, s32[]{:T(128)} %constant.647.clone.1, s32[]{:T(128)} %constant.647.clone.1, s32[]{:T(128)} %constant.651.clone.1, s32[]{:T(128)} %constant.647.clone.1, s32[]{:T(128)} %constant.647.clone.1, s32[]{:T(128)} %constant.647.clone.1) | dynamic-update-slice | bytes 270340 | tf_op jit(solution)/shard_map/scatter | solution.py:106
  740.9 14.8 %scatter.139 = f32[32,3,11,11,1,32]{5,2,3,1,0,4:T(8,128)} dynamic-update-slice(f32[32,3,11,11,1,32]{5,2,3,1,0,4:T(8,128)} %scatter.136, f32[32,3,1,11,1,32]{5,2,3,1,0,4:T(1,128)S(1)} %copy.462, s32[]{:T(128)} %constant.647.clone.1, s32[]{:T(128)} %constant.647.clone.1, s32[]{:T(128)} %constant.647.clone.1, s32[]{:T(128)} %constant.647.clone.1, s32[]{:T(128)} %constant.647.clone.1, s32[]{:T(128)} %constant.647.clone.1) | dynamic-update-slice | bytes 270340 | tf_op jit(solution)/shard_map/scatter | solution.py:106
  755.7 18.9 %add_add_fusion = f32[32,3,11,11,1,32]{5,2,3,1,0,4:T(8,128)S(1)} fusion(f32[32,3,11,11,1,32]{5,2,3,1,0,4:T(8,128)} %get-tuple-element.342, f32[32,3,11,11,1,32]{5,2,3,1,0,4:T(8,128)} %scatter.139, f32[32,3,11,11,1,32]{5,2,3,1,0,4:T(8,128)} %copy-done, f32[32,3,11,11,1,32]{5,2,3,1,0,4:T(8,128)} %copy-done.3, f32[32,3,11,11,1,32]{5,2,3,1,0,4:T(8,128)} %copy-done.2, ...), kind=kLoop, calls=%fused_computation.32 | loop fusion | flops 5203968 | bytes 11894784 | tf_op jit(solution)/shard_map/add | solution.py:138
  774.7 7.2 copy.463
  (138 shorter events, 74.3 us)
Async XLA Ops:
  0.0 7.2 copy-start.15
  0.0 7.2 copy-start.9
  33.2 32.9 %copy-start.10 = (f32[11,11]{1,0:T(8,128)S(1)}, f32[11,11]{1,0:T(8,128)}, u32[]{:S(2)}) copy-start(f32[11,11]{1,0:T(8,128)} %constant.668.clone) | copy-start | bytes 1456
  33.2 33.6 %copy-start.14 = (f32[11]{0:T(128)S(1)}, f32[11]{0:T(128)}, u32[]{:S(2)}) copy-start(f32[11]{0:T(128)} %constant.667.clone) | copy-start | bytes 136
  33.2 33.9 %copy-start.13 = (f32[11,11,1,32]{3,2,1,0:T(1,128)S(1)}, f32[11,11,1,32]{3,2,1,0:T(1,128)}, u32[]{:S(2)}) copy-start(f32[11,11,1,32]{3,2,1,0:T(1,128)} %param.62) | copy-start | bytes 46468
  60.3 36.1 %all-to-all-start = ((f32[16,1,23232]{2,1,0:T(1,128)}), f32[16,1,23232]{2,1,0:T(1,128)}, u32[]{:S(2)}, u32[]{:S(2)}) async-start(f32[16,1,23232]{2,1,0:T(1,128)} %reshape.1472), calls=%async_computation | async-start | bytes 2981888 | tf_op jit(solution)/shard_map/all_to_all | solution.py:157
  71.4 16.6 %collective-permute-start = (f32[32,1,11,32]{3,1,2,0:T(1,128)S(1)}, f32[32,1,11,32]{3,1,2,0:T(1,128)S(1)}, u32[]{:S(2)}, u32[]{:S(2)}) collective-permute-start(f32[32,1,11,32]{3,1,2,0:T(1,128)S(1)} %get-tuple-element.379), channel_id=1, source_target_pairs={{1,0},{2,1},{3,2},{4,3},{5,4},{6,5},{7,6},{9,8},{10,9},{11,10},{12... | collective-permute-start | bytes 135176 | tf_op jit(solution)/shard_map/ppermute | solution.py:23
  74.1 12.1 %collective-permute-start.1 = (f32[32,1,11,32]{3,1,2,0:T(1,128)S(1)}, f32[32,1,11,32]{3,1,2,0:T(1,128)S(1)}, u32[]{:S(2)}, u32[]{:S(2)}) collective-permute-start(f32[32,1,11,32]{3,1,2,0:T(1,128)S(1)} %get-tuple-element.380), channel_id=1, source_target_pairs={{0,1},{1,2},{2,3},{3,4},{4,5},{5,6},{6,7},{8,9},{9,10},{10,11},{11... | collective-permute-start | bytes 135176 | tf_op jit(solution)/shard_map/ppermute | solution.py:23
  83.0 294.3 %copy-start.4 = (f32[32,11,11,32]{3,1,2,0:T(8,128)}, f32[32,11,11,32]{3,1,2,0:T(8,128)S(1)}, u32[]{:S(2)}) copy-start(f32[32,11,11,32]{3,1,2,0:T(8,128)S(1)} %get-tuple-element.385) | copy-start | bytes 1486852
  187.6 7.4 copy-start.11
  188.8 3.4 copy-start.1
  193.0 18.8 %collective-permute-start.2 = (f32[32,3,11,32]{3,0,2,1:T(8,128)S(1)}, f32[32,3,11,32]{3,0,2,1:T(8,128)S(1)}, u32[]{:S(2)}, u32[]{:S(2)}) collective-permute-start(f32[32,3,11,32]{3,0,2,1:T(8,128)S(1)} %bitcast.399), channel_id=1, source_target_pairs={{1,0},{2,1},{3,2},{4,3},{5,4},{6,5},{7,6},{9,8},{10,9},{11,10},{12... | collective-permute-start | bytes 405512 | tf_op jit(solution)/shard_map/ppermute | solution.py:23
  201.7 18.0 %collective-permute-start.3 = (f32[32,3,11,32]{3,0,2,1:T(8,128)S(1)}, f32[32,3,11,32]{3,0,2,1:T(8,128)S(1)}, u32[]{:S(2)}, u32[]{:S(2)}) collective-permute-start(f32[32,3,11,32]{3,0,2,1:T(8,128)S(1)} %bitcast.403), channel_id=1, source_target_pairs={{0,1},{1,2},{2,3},{3,4},{4,5},{5,6},{6,7},{8,9},{9,10},{10,11},{11... | collective-permute-start | bytes 405512 | tf_op jit(solution)/shard_map/ppermute | solution.py:23
  251.2 5.2 copy-start.12
  302.1 18.3 %collective-permute-start.4 = (f32[32,3,11,32]{3,0,2,1:T(8,128)S(1)}, f32[32,3,11,32]{3,0,2,1:T(8,128)S(1)}, u32[]{:S(2)}, u32[]{:S(2)}) collective-permute-start(f32[32,3,11,32]{3,0,2,1:T(8,128)S(1)} %bitcast.404), channel_id=1, source_target_pairs={{1,0},{2,1},{3,2},{4,3},{5,4},{6,5},{7,6},{9,8},{10,9},{11,10},{12... | collective-permute-start | bytes 405512 | tf_op jit(solution)/shard_map/ppermute | solution.py:23
  304.9 32.0 %collective-permute-start.5 = (f32[32,3,11,32]{3,0,2,1:T(8,128)}, f32[32,3,11,32]{3,0,2,1:T(8,128)}, u32[]{:S(2)}, u32[]{:S(2)}) collective-permute-start(f32[32,3,11,32]{3,0,2,1:T(8,128)} %bitcast.371), channel_id=1, source_target_pairs={{0,1},{1,2},{2,3},{3,4},{4,5},{5,6},{6,7},{8,9},{9,10},{10,11},{11... | collective-permute-start | bytes 405512 | tf_op jit(solution)/shard_map/ppermute | solution.py:23
  365.6 11.7 %copy-start.2 = (f32[32,3,11,11,1,32]{5,2,3,1,0,4:T(8,128)}, f32[32,3,11,11,1,32]{5,2,3,1,0,4:T(8,128)S(1)}, u32[]{:S(2)}) copy-start(f32[32,3,11,11,1,32]{5,2,3,1,0,4:T(8,128)S(1)} %get-tuple-element.347) | copy-start | bytes 4460548
  400.2 16.9 %collective-permute-start.6 = (f32[32,3,11,32]{3,0,2,1:T(8,128)S(1)}, f32[32,3,11,32]{3,0,2,1:T(8,128)S(1)}, u32[]{:S(2)}, u32[]{:S(2)}) collective-permute-start(f32[32,3,11,32]{3,0,2,1:T(8,128)S(1)} %bitcast.405), channel_id=1, source_target_pairs={{1,0},{2,1},{3,2},{4,3},{5,4},{6,5},{7,6},{9,8},{10,9},{11,10},{12... | collective-permute-start | bytes 405512 | tf_op jit(solution)/shard_map/ppermute | solution.py:23
  402.2 30.9 %collective-permute-start.7 = (f32[32,3,11,32]{3,0,2,1:T(8,128)S(1)}, f32[32,3,11,32]{3,0,2,1:T(8,128)S(1)}, u32[]{:S(2)}, u32[]{:S(2)}) collective-permute-start(f32[32,3,11,32]{3,0,2,1:T(8,128)S(1)} %bitcast.400), channel_id=1, source_target_pairs={{0,1},{1,2},{2,3},{3,4},{4,5},{5,6},{6,7},{8,9},{9,10},{10,11},{11... | collective-permute-start | bytes 405512 | tf_op jit(solution)/shard_map/ppermute | solution.py:23
  462.3 11.8 %copy-start.3 = (f32[32,3,11,11,1,32]{5,2,3,1,0,4:T(8,128)}, f32[32,3,11,11,1,32]{5,2,3,1,0,4:T(8,128)S(1)}, u32[]{:S(2)}) copy-start(f32[32,3,11,11,1,32]{5,2,3,1,0,4:T(8,128)S(1)} %get-tuple-element.345) | copy-start | bytes 4460548
  462.3 11.8 %copy-start.5 = (f32[32,11,11,32]{3,1,2,0:T(8,128)S(1)}, f32[32,11,11,32]{3,1,2,0:T(8,128)}, u32[]{:S(2)}) copy-start(f32[32,11,11,32]{3,1,2,0:T(8,128)} %copy-done.4) | copy-start | bytes 1486852
  497.8 16.0 %collective-permute-start.8 = (f32[32,3,11,32]{3,0,2,1:T(8,128)S(1)}, f32[32,3,11,32]{3,0,2,1:T(8,128)S(1)}, u32[]{:S(2)}, u32[]{:S(2)}) collective-permute-start(f32[32,3,11,32]{3,0,2,1:T(8,128)S(1)} %bitcast.406), channel_id=1, source_target_pairs={{1,0},{2,1},{3,2},{4,3},{5,4},{6,5},{7,6},{9,8},{10,9},{11,10},{12... | collective-permute-start | bytes 405512 | tf_op jit(solution)/shard_map/ppermute | solution.py:23
  499.8 29.5 %collective-permute-start.9 = (f32[32,3,11,32]{3,0,2,1:T(8,128)S(1)}, f32[32,3,11,32]{3,0,2,1:T(8,128)S(1)}, u32[]{:S(2)}, u32[]{:S(2)}) collective-permute-start(f32[32,3,11,32]{3,0,2,1:T(8,128)S(1)} %bitcast.401), channel_id=1, source_target_pairs={{0,1},{1,2},{2,3},{3,4},{4,5},{5,6},{6,7},{8,9},{9,10},{10,11},{11... | collective-permute-start | bytes 405512 | tf_op jit(solution)/shard_map/ppermute | solution.py:23
  558.5 11.7 %copy-start = (f32[32,3,11,11,1,32]{5,2,3,1,0,4:T(8,128)}, f32[32,3,11,11,1,32]{5,2,3,1,0,4:T(8,128)S(1)}, u32[]{:S(2)}) copy-start(f32[32,3,11,11,1,32]{5,2,3,1,0,4:T(8,128)S(1)} %get-tuple-element.343) | copy-start | bytes 4460548
  558.5 11.7 %copy-start.6 = (f32[32,11,11,32]{3,1,2,0:T(8,128)S(1)}, f32[32,11,11,32]{3,1,2,0:T(8,128)}, u32[]{:S(2)}) copy-start(f32[32,11,11,32]{3,1,2,0:T(8,128)} %copy-done.4) | copy-start | bytes 1486852
  594.0 15.1 %collective-permute-start.10 = (f32[32,3,11,32]{3,0,2,1:T(8,128)S(1)}, f32[32,3,11,32]{3,0,2,1:T(8,128)S(1)}, u32[]{:S(2)}, u32[]{:S(2)}) collective-permute-start(f32[32,3,11,32]{3,0,2,1:T(8,128)S(1)} %bitcast.407), channel_id=1, source_target_pairs={{1,0},{2,1},{3,2},{4,3},{5,4},{6,5},{7,6},{9,8},{10,9},{11,10},{12... | collective-permute-start | bytes 405512 | tf_op jit(solution)/shard_map/ppermute | solution.py:23
  596.0 28.5 %collective-permute-start.11 = (f32[32,3,11,32]{3,0,2,1:T(8,128)S(1)}, f32[32,3,11,32]{3,0,2,1:T(8,128)S(1)}, u32[]{:S(2)}, u32[]{:S(2)}) collective-permute-start(f32[32,3,11,32]{3,0,2,1:T(8,128)S(1)} %bitcast.402), channel_id=1, source_target_pairs={{0,1},{1,2},{2,3},{3,4},{4,5},{5,6},{6,7},{8,9},{9,10},{10,11},{11... | collective-permute-start | bytes 405512 | tf_op jit(solution)/shard_map/ppermute | solution.py:23
  674.5 6.4 copy-start.7
  701.3 54.4 %copy-start.8 = (f32[32,11,11,32]{3,1,2,0:T(8,128)S(1)}, f32[32,11,11,32]{3,1,2,0:T(8,128)}, u32[]{:S(2)}) copy-start(f32[32,11,11,32]{3,1,2,0:T(8,128)} %get-tuple-element.378) | copy-start | bytes 1486852
  708.1 14.9 %collective-permute-start.12 = (f32[32,3,11,32]{3,0,2,1:T(8,128)S(1)}, f32[32,3,11,32]{3,0,2,1:T(8,128)S(1)}, u32[]{:S(2)}, u32[]{:S(2)}) collective-permute-start(f32[32,3,11,32]{3,0,2,1:T(8,128)S(1)} %bitcast.408), channel_id=1, source_target_pairs={{1,0},{2,1},{3,2},{4,3},{5,4},{6,5},{7,6},{9,8},{10,9},{11,10},{12... | collective-permute-start | bytes 405512 | tf_op jit(solution)/shard_map/ppermute | solution.py:23
  710.9 28.3 %collective-permute-start.13 = (f32[32,3,11,32]{3,0,2,1:T(8,128)}, f32[32,3,11,32]{3,0,2,1:T(8,128)}, u32[]{:S(2)}, u32[]{:S(2)}) collective-permute-start(f32[32,3,11,32]{3,0,2,1:T(8,128)} %bitcast.363), channel_id=1, source_target_pairs={{0,1},{1,2},{2,3},{3,4},{4,5},{5,6},{6,7},{8,9},{9,10},{10,11},{11... | collective-permute-start | bytes 405512 | tf_op jit(solution)/shard_map/ppermute | solution.py:23
where the time goes:
time: 796 us; the launch traced here: 782 us
  local copies, waits for them, and re-layouts  370 us (46%)
  matrix products  147 us (18%)
  other arithmetic  145 us (18%)
  starting transfers between devices  72.5 us (9%)
  waiting for transfers between devices  46 us (6%)
    scatter x14, local copies, waits for them, and re-layouts, assemble(): return field.at[:, :, -1].set(right_new).at[:, :, 0].set(left_new)  187 us
    dot_general x5, matrix products, helm_apply(): jnp.einsum('ia,rcabxy->rcibxy', stiff_mat, field, precision=lax.Precision...  77.8 us
    unnamed x36, local copies, waits for them, and re-layouts  66.8 us
    ppermute x14, starting transfers between devices, shifted(): return lax.ppermute(array, axis, pairs)  66.7 us
    dot_general x5, matrix products, helm_apply(): jnp.einsum('jb,rcabxy->rcajxy', stiff_mat, field, precision=lax.Precision...  58.9 us
    ppermute x14, waiting for transfers between devices, shifted(): return lax.ppermute(array, axis, pairs)  46 us
    all_to_all x4, local copies, waits for them, and re-layouts, per_device(): lax.all_to_all(spectra, 'mode', split_axis=0, concat_axis=5, tiled=True)  44.2 us
    add x3, other arithmetic, chebyshev(): recurrence_next * recurrence * direction  39.7 us
  transfers between devices with their start and end apart: 15, of which 9 were waited for; matrix products, arithmetic and copies ran while one was open for 13% of the time, Pallas kernels for 0%

commit v1 on v0

v1 whole, which is shorter than its diff:
```python
import functools
import math

import jax
import jax.numpy as jnp
import ml_dtypes
import numpy as np
from jax import lax
from jax.experimental import pallas as pl
from jax.experimental.pallas import tpu as pltpu
from jax.sharding import PartitionSpec as P

ORDER = 10
NQ = ORDER + 1
NODES = NQ * NQ
PLANES = 512
MODES = 256
ITERS = 6
HELM_BASE = 1.0
SPAN_WAVE = 0.02
BOUND_RATIO = 25.0

COMPS = 3
PADDED = 128
OWNERS = 16
COLUMNS = 8
GROUPS = 2 * COMPS
HALF = ORDER // 2
MESH = pl.DeviceIdType.MESH
VMEM_LIMIT = 56 * 2**20


def legendre_pair(points, order):
    previous = points * 0.0 + 1.0
    current = points * 1.0
    for degree in range(2, order + 1):
        following = ((2 * degree - 1) * points * current - (degree - 1) * previous) / degree
        previous = current
        current = following
    return (current, previous)


def gll_tables(order):
    count = order + 1
    points = -np.cos(np.pi * np.arange(count) / order)
    for sweep in range(200):
        top_vals, below_vals = legendre_pair(points, order)
        points = points - (points * top_vals - below_vals) / (count * top_vals)
    legendre_vals, below_vals = legendre_pair(points, order)
    weights = 2.0 / (order * (order + 1) * legendre_vals**2)
    identity = np.eye(count)
    spacing = points[:, None] - points[None, :] + identity
    derivative = legendre_vals[:, None] / (legendre_vals[None, :] * spacing) * (1.0 - identity)
    corner = np.concatenate(
        [[-order * (order + 1) / 4.0], np.zeros(order - 1), [order * (order + 1) / 4.0]]
    )
    derivative = derivative + identity * corner[None, :]
    stiffness = derivative.T @ (weights[:, None] * derivative)
    weight_mat = identity * weights[None, :]
    laplace = np.kron(stiffness, weight_mat) + np.kron(weight_mat, stiffness)
    upper_bound = float(
        np.max(np.sum(np.abs(laplace), axis=1) / np.sum(laplace * np.eye(count * count), axis=1))
    )
    return weights, stiffness, derivative, upper_bound


WEIGHTS, STIFF, DERIV, TOP = gll_tables(ORDER)
SCALED = STIFF / WEIGHTS[:, None]


def chebyshev_table():
    low = TOP / BOUND_RATIO
    mid = (TOP + low) / 2.0
    half = (TOP - low) / 2.0
    table = [(0.0, 1.0 / mid)]
    recurrence = half / mid
    for step in range(ITERS - 1):
        following = 1.0 / (2.0 * mid / half - recurrence)
        table.append((following * recurrence, 2.0 * following / half))
        recurrence = following
    return np.asarray(table, np.float32).T.copy()


def dft_table():
    planes = np.arange(PLANES)
    modes = np.arange(MODES)
    angles = 2.0 * np.pi / PLANES * (modes[:, None] * planes[None, :] % PLANES)
    table = np.concatenate([np.cos(angles), -np.sin(angles)]) / math.sqrt(PLANES)
    high = table.astype(ml_dtypes.bfloat16)
    low = (table - high.astype(np.float64)).astype(ml_dtypes.bfloat16)
    return high, low


def lines(vals, matrix, sign):
    evens = [vals[k] + vals[ORDER - k] for k in range(HALF)]
    odds = [vals[k] - vals[ORDER - k] for k in range(HALF)]
    out = [None] * NQ
    for i in range(HALF):
        even = vals[HALF] * float(matrix[i, HALF])
        odd = None
        for k in range(HALF):
            even = even + evens[k] * float((matrix[i, k] + matrix[i, ORDER - k]) / 2)
            term = odds[k] * float((matrix[i, k] - matrix[i, ORDER - k]) / 2)
            odd = term if odd is None else odd + term
        out[i] = even + odd
        out[ORDER - i] = even - odd if sign > 0 else odd - even
    middle = vals[HALF] * float(matrix[HALF, HALF]) if sign > 0 else None
    for k in range(HALF):
        term = (evens if sign > 0 else odds)[k] * float(matrix[HALF, k])
        middle = term if middle is None else middle + term
    out[HALF] = middle
    return out


def roll(tile, by):
    return pltpu.roll(tile, by % 128, 1)


def forward_kernel(vel, high, low, out, tmp, forcing):
    forcing[pl.ds(NODES * 8, (PADDED - NODES) * 8), :] = jnp.zeros(
        ((PADDED - NODES) * 8, 128), jnp.float32
    )

    for c in range(COMPS):

        def first(b, _):
            grads = lines([vel[c * NODES + a * NQ + b] for a in range(NQ)], DERIV, -1)
            for a in range(NQ):
                tmp[a * NQ + b] = vel[a * NQ + b] * grads[a]
            return 0

        def second(a, _):
            vals = [vel[c * NODES + a * NQ + b] for b in range(NQ)]
            grads = lines(vals, DERIV, -1)
            for b in range(NQ):
                node = a * NQ + b
                value = vals[b] - (tmp[node] + vel[NODES + node] * grads[b])
                forcing[pl.ds(pl.multiple_of(node * 8, 8), 8), :] = value
            return 0

        lax.fori_loop(0, NQ, first, 0)
        lax.fori_loop(0, NQ, second, 0)
        for g in range(2):
            field = jnp.concatenate(
                [
                    jnp.concatenate(
                        [forcing[pl.ds(g * 512 + t * 2 + y, 64, stride=8), :] for y in range(2)],
                        axis=0,
                    )
                    for t in range(4)
                ],
                axis=1,
            )
            upper = field.astype(jnp.bfloat16)
            lower = (field - upper.astype(jnp.float32)).astype(jnp.bfloat16)
            dims = (((1,), (1,)), ((), ()))
            dot = functools.partial(
                lax.dot_general, dimension_numbers=dims, preferred_element_type=jnp.float32
            )
            spectra = dot(high[...], upper) + (dot(high[...], lower) + dot(low[...], upper))
            out[:, c * 2 + g] = spectra.reshape(OWNERS, 4, 8, 128)


def forward(velocity):
    tiles = velocity.reshape(COMPS * NODES, 2, 4, 128).transpose(0, 2, 1, 3)
    tiles = tiles.reshape(COMPS * NODES, 8, 128)
    high, low = dft_table()
    return pl.pallas_call(
        forward_kernel,
        out_shape=jax.ShapeDtypeStruct((OWNERS, GROUPS, 4, 8, 128), jnp.float32),
        scratch_shapes=[
            pltpu.VMEM((NODES, 8, 128), jnp.float32),
            pltpu.VMEM((PADDED * 8, 128), jnp.float32),
        ],
        compiler_params=pltpu.CompilerParams(vmem_limit_bytes=VMEM_LIMIT),
        name="forward",
    )(tiles, jnp.asarray(high), jnp.asarray(low))


def exchange_kernel(src, dst, send_sem, recv_sem, local_sem):
    me, column = lax.axis_index("mode"), lax.axis_index("mesh")
    barrier = pltpu.get_barrier_semaphore()
    for offset in range(1, OWNERS):
        pl.semaphore_signal(
            barrier,
            inc=1,
            device_id=(lax.rem(me + offset, OWNERS), column),
            device_id_type=MESH,
        )
    pl.semaphore_wait(barrier, OWNERS - 1)
    copies = []
    for offset in range(1, OWNERS):
        dest = lax.rem(me + offset, OWNERS)
        copy = pltpu.make_async_remote_copy(
            src_ref=src.at[dest],
            dst_ref=dst.at[me],
            send_sem=send_sem.at[offset],
            recv_sem=recv_sem.at[offset],
            device_id=(dest, column),
            device_id_type=MESH,
        )
        copy.start()
        copies.append(copy)
    local = pltpu.make_async_copy(src.at[me], dst.at[me], local_sem)
    local.start()
    local.wait()
    for copy in copies:
        copy.wait()


def exchange(spectra):
    return pl.pallas_call(
        exchange_kernel,
        out_shape=jax.ShapeDtypeStruct(spectra.shape, spectra.dtype),
        in_specs=[pl.BlockSpec(memory_space=pl.ANY)],
        out_specs=pl.BlockSpec(memory_space=pl.ANY),
        scratch_shapes=[
            pltpu.SemaphoreType.DMA((OWNERS,)),
            pltpu.SemaphoreType.DMA((OWNERS,)),
            pltpu.SemaphoreType.DMA,
        ],
        compiler_params=pltpu.CompilerParams(collective_id=0, has_side_effects=True),
        name="exchange",
    )(spectra)


def lane_bits():
    lane = lax.broadcasted_iota(jnp.int32, (8, 128), 1)
    return lane, lane // 64, lane // 16 % 4, lane % 16


def join_rows(low, high):
    _, parity, _, pair = lane_bits()
    above = jnp.where(parity == 0, roll(low, 64), roll(low, 63))
    below = jnp.where(parity == 1, roll(high, 64), roll(high, 65))
    last = (parity == 1) & (pair == 15)
    first = (parity == 0) & (pair == 0)
    return low + jnp.where(first, 0.0, below), high + jnp.where(last, 0.0, above)


def butterfly(tiles, first_bit):
    tiles = list(tiles)
    lane = lax.broadcasted_iota(jnp.int32, (8, 128), 1)
    for bit in range(3):
        width = 1 << (first_bit + bit)
        upper = lane // width % 2 == 1
        for i in range(8):
            if i >> bit & 1 == 0:
                j = i | 1 << bit
                a, b = tiles[i], tiles[j]
                tiles[i] = jnp.where(upper, roll(b, width), a)
                tiles[j] = jnp.where(upper, b, roll(a, -width))
    return tiles


def solve_kernel(
    spectra,
    penalty,
    laplace,
    table,
    out,
    res,
    direction,
    tmp,
    inverse,
    coeff,
    swap,
    sent,
    got,
    pen_sent,
    pen_got,
    send_sem,
    recv_sem,
    pen_send_sem,
    pen_recv_sem,
):
    mode, column = lax.axis_index("mode"), lax.axis_index("mesh")
    has = (column > 0, column < COLUMNS - 1)
    partner = (jnp.maximum(column - 1, 0), jnp.minimum(column + 1, COLUMNS - 1))
    edge_rows = (0, ORDER)

    def face_copy(step, c, side):
        return pltpu.make_async_remote_copy(
            src_ref=sent.at[step, c, side],
            dst_ref=got.at[step, c, 1 - side],
            send_sem=send_sem.at[step, c, side],
            recv_sem=recv_sem.at[step, c, 1 - side],
            device_id=(mode, partner[side]),
            device_id_type=MESH,
        )

    def pen_copy(side):
        return pltpu.make_async_remote_copy(
            src_ref=pen_sent.at[side],
            dst_ref=pen_got.at[1 - side],
            send_sem=pen_send_sem.at[side],
            recv_sem=pen_recv_sem.at[1 - side],
            device_id=(mode, partner[side]),
            device_id_type=MESH,
        )

    def start_faces(step, c):
        for side in range(2):

            @pl.when(has[side])
            def _():
                face_copy(step, c, side).start()

    def wait_faces(step, c):
        for side in range(2):

            @pl.when(has[side])
            def _():
                face_copy(step, c, side).wait_send()
                face_copy(step, c, 1 - side).wait_recv()

    for side in range(2):

        @pl.when(jnp.logical_not(has[side]))
        def _():
            for step in range(ITERS):
                got[step, :, side] = jnp.zeros((COMPS, NQ, 8, 128), jnp.float32)

    barrier = pltpu.get_barrier_semaphore()
    for side in range(2):

        @pl.when(has[side])
        def _():
            pl.semaphore_signal(
                barrier, inc=1, device_id=(mode, partner[side]), device_id_type=MESH
            )

    pl.semaphore_wait(barrier, has[0].astype(jnp.int32) + has[1].astype(jnp.int32))

    for side in range(2):
        pen_sent[side] = penalty[pl.ds(edge_rows[side] * NQ, 16), :]

        @pl.when(has[side])
        def _():
            pen_copy(side).start()

    def unpack(group, _):
        def low_bits(i, _):
            block, source = i // 2, (i % 2) * 8
            tiles = butterfly([spectra[source + k, group, block] for k in range(8)], 0)
            for k in range(8):
                swap[i * 8 + k] = tiles[k]
            return 0

        def high_bits(j, _):
            tiles = butterfly([swap[h * 8 + j] for h in range(8)], 3)
            for h in range(8):
                res[group * 64 + h * 8 + j] = tiles[h]
            return 0

        lax.fori_loop(0, 8, low_bits, 0)
        lax.fori_loop(0, 8, high_bits, 0)
        return 0

    lax.fori_loop(0, GROUPS, unpack, 0)

    for c in range(COMPS):

        def join_rhs(a, _):
            node = c * PADDED + a * NQ
            low, high = join_rows(res[node], res[node + ORDER])
            res[node] = low
            res[node + ORDER] = high
            return 0

        lax.fori_loop(0, NQ, join_rhs, 0)
        zero = jnp.zeros((8, 128), jnp.float32)
        for side in range(2):
            for b in range(NQ):
                node = c * PADDED + edge_rows[side] * NQ + b
                sent[0, c, side, b] = -res[node]
                res[node] = zero
                direction[node] = zero
                out[node] = zero
        start_faces(0, c)

    _, _, block, _ = lane_bits()
    row = mode * 32 + block * 8 + lax.broadcasted_iota(jnp.int32, (8, 128), 0)
    wave = (row % MODES).astype(jnp.float32)
    helm = HELM_BASE + (SPAN_WAVE * wave) * (SPAN_WAVE * wave)

    def make_coeff(node, _):
        value = helm + penalty[pl.ds(node, 1), :]
        coeff[node] = value
        inverse[node] = value + laplace[pl.ds(node, 1), :]
        return 0

    lax.fori_loop(0, NODES, make_coeff, 0)
    for side in range(2):

        @pl.when(has[side])
        def _():
            pen_copy(side).wait_send()
            pen_copy(1 - side).wait_recv()
            for b in range(NQ):
                node = edge_rows[side] * NQ + b
                other = helm + pen_got[side, pl.ds(b, 1), :]
                inverse[node] += other + laplace[pl.ds(node, 1), :]

    def invert(a, _):
        vals = [inverse[a * NQ + b] for b in range(NQ)]
        vals[0], vals[ORDER] = join_rows(vals[0], vals[ORDER])
        for b in range(NQ):
            inverse[a * NQ + b] = 1.0 / vals[b]
        return 0

    lax.fori_loop(0, NQ, invert, 0)

    for c in range(COMPS):

        def begin(i, _):
            node = NQ + i
            value = inverse[node] * res[c * PADDED + node] * table[1, 0]
            direction[c * PADDED + node] = value
            out[c * PADDED + node] = value
            return 0

        lax.fori_loop(0, NODES - 2 * NQ, begin, 0)

    def update(base, node, change, keep, gain):
        now = res[base + node] - change
        res[base + node] = now
        value = keep * direction[base + node] + gain * (inverse[node] * now)
        direction[base + node] = value
        out[base + node] += value

    def finish_faces(step, c):
        wait_faces(step, c)
        keep, gain = table[0, step], table[1, step]
        for side in range(2):
            for b in range(NQ):
                change = sent[step, c, side, b] + got[step, c, side, b]
                update(c * PADDED, edge_rows[side] * NQ + b, change, keep, gain)

    def along_second(base, a):
        terms = lines([direction[base + a * NQ + b] for b in range(NQ)], SCALED, 1)
        terms = [terms[b] + tmp[a * NQ + b] for b in range(NQ)]
        terms[0], terms[ORDER] = join_rows(terms[0], terms[ORDER])
        return terms

    def sweep(q, _):
        step, c = q // COMPS, q % COMPS
        base = c * PADDED
        finish_faces(step, c)

        def along_first(b, _):
            vals = [direction[base + a * NQ + b] for a in range(NQ)]
            terms = lines(vals, SCALED, 1)
            for a in range(NQ):
                tmp[a * NQ + b] = terms[a] + coeff[a * NQ + b] * vals[a]
            return 0

        lax.fori_loop(0, NQ, along_first, 0)
        for side in range(2):
            terms = along_second(base, edge_rows[side])
            for b in range(NQ):
                sent[step + 1, c, side, b] = terms[b]
        start_faces(step + 1, c)
        keep, gain = table[0, step + 1], table[1, step + 1]

        def interior(a, _):
            terms = along_second(base, a)
            for b in range(NQ):
                update(base, a * NQ + b, terms[b], keep, gain)
            return 0

        lax.fori_loop(1, ORDER, interior, 0)
        return 0

    lax.fori_loop(0, (ITERS - 1) * COMPS, sweep, 0)
    for c in range(COMPS):
        finish_faces(ITERS - 1, c)


def solve(spectra, penalty):
    pen = penalty.reshape(NODES, 16, 2).transpose(0, 2, 1)
    pen = jnp.broadcast_to(pen[:, :, None, :], (NODES, 2, 4, 16)).reshape(NODES, 128)
    pen = jnp.pad(pen, ((0, PADDED - NODES), (0, 0)))
    diag = np.diagonal(SCALED)
    laplace = np.zeros((PADDED, 128), np.float32)
    laplace[:NODES] = (diag[:, None] + diag[None, :]).reshape(NODES, 1)
    tile = (8, 128)
    vmem = pl.BlockSpec(memory_space=pltpu.VMEM)
    return pl.pallas_call(
        solve_kernel,
        out_shape=jax.ShapeDtypeStruct((COMPS * PADDED,) + tile, jnp.float32),
        in_specs=[vmem, vmem, vmem, pl.BlockSpec(memory_space=pltpu.SMEM)],
        out_specs=vmem,
        scratch_shapes=[
            pltpu.VMEM((COMPS * PADDED,) + tile, jnp.float32),
            pltpu.VMEM((COMPS * PADDED,) + tile, jnp.float32),
            pltpu.VMEM((PADDED,) + tile, jnp.float32),
            pltpu.VMEM((PADDED,) + tile, jnp.float32),
            pltpu.VMEM((PADDED,) + tile, jnp.float32),
            pltpu.VMEM((64,) + tile, jnp.float32),
            pltpu.VMEM((ITERS, COMPS, 2, NQ) + tile, jnp.float32),
            pltpu.VMEM((ITERS, COMPS, 2, NQ) + tile, jnp.float32),
            pltpu.VMEM((2, 16, 128), jnp.float32),
            pltpu.VMEM((2, 16, 128), jnp.float32),
            pltpu.SemaphoreType.DMA((ITERS, COMPS, 2)),
            pltpu.SemaphoreType.DMA((ITERS, COMPS, 2)),
            pltpu.SemaphoreType.DMA((2,)),
            pltpu.SemaphoreType.DMA((2,)),
        ],
        compiler_params=pltpu.CompilerParams(
            collective_id=1, has_side_effects=True, vmem_limit_bytes=VMEM_LIMIT
        ),
        name="solve",
    )(spectra, pen, jnp.asarray(laplace), jnp.asarray(chebyshev_table()))


def unpack_kernel(tiles, out):
    block = pl.program_id(0)
    lane = lax.broadcasted_iota(jnp.int32, (8, 128), 1)
    source = (lane % 2) * 64 + block * 16 + lane // 2 % 16
    for c in range(COMPS):

        def one(node, _):
            rows = jnp.take_along_axis(tiles[c * PADDED + node], source, axis=1)
            out[pl.ds(c * NODES + node, 8, stride=COMPS * NODES), :] = rows[:, :32]
            return 0

        lax.fori_loop(0, NODES, one, 0, unroll=11)


def unpack_output(tiles):
    rows = 8 * COMPS * NODES
    out = pl.pallas_call(
        unpack_kernel,
        grid=(4,),
        out_shape=jax.ShapeDtypeStruct((4 * rows, 32), jnp.float32),
        in_specs=[pl.BlockSpec(memory_space=pltpu.VMEM)],
        out_specs=pl.BlockSpec((rows, 32), lambda i: (i, 0)),
        compiler_params=pltpu.CompilerParams(vmem_limit_bytes=VMEM_LIMIT),
        name="unpack",
    )(tiles)
    return out.reshape(32, COMPS, NQ, NQ, 1, 32)


def per_device(velocity, penalty):
    return unpack_output(solve(exchange(forward(velocity)), penalty))


def solution(mesh):
    return jax.shard_map(
        per_device,
        mesh=mesh,
        in_specs=(P(None, None, None, "mesh", "mode", None), P(None, None, "mesh", None)),
        out_specs=P("mode", None, None, None, "mesh", None),
        check_vma=False,
    )
```

time: 796 us -> 114 us (0.14)
  the two profiles are of different devices: /device:TPU:24 before, /device:TPU:96 now
where the time goes in v1:
time: 114 us; the launch traced here: 112 us
  Pallas kernels  110 us (96%)
  local copies, waits for them, and re-layouts  1.9 us (2%)
    pallas_call x1, Pallas kernels, solve(): pl.pallas_call(solve_kernel, out_shape=jax.ShapeDtypeStruct((COMPS * PADD...  63.7 us
    pallas_call x1, Pallas kernels, exchange(): pl.pallas_call(exchange_kernel, out_shape=jax.ShapeDtypeStruct(spectra.sh...  25.9 us
    pallas_call x1, Pallas kernels, unpack_output(): pl.pallas_call(unpack_kernel, grid=(4,), out_shape=jax.ShapeDtypeStruct((...  13.3 us
    pallas_call x1, Pallas kernels, forward(): pl.pallas_call(forward_kernel, out_shape=jax.ShapeDtypeStruct((OWNERS, GR...  7.51 us

profile of v1, /device:TPU:96, one launch (start us, length us, event | category | flops | bytes accessed | tf_op | source)
XLA Modules:
  0.0 112.4 jit_solution(4303109857610968789)
XLA Ops:
  0.0 1.0 copy.11
  1.0 0.1 reshape.18
  1.2 0.1 copy.13
  1.3 0.6 pad.4.penalty
  1.9 7.5 %forward.1.src = f32[16,6,4,8,128]{4,3,2,1,0:T(8,128)} custom-call(f32[363,8,128]{2,1,0:T(8,128)} %bitcast.10, bf16[512,512]{1,0:T(8,128)(2,1)} %constant.11.clone.high, bf16[512,512]{1,0:T(8,128)(2,1)} %constant.12.clone.low), custom_call_target="tpu_custom_call" | custom-call | tf_op jit(solution)/shard_map/forward/pallas_call | solution.py:168
  9.4 25.9 %exchange.1.spectra = f32[16,6,4,8,128]{4,3,2,1,0:T(8,128)} custom-call(f32[16,6,4,8,128]{4,3,2,1,0:T(8,128)} %forward.1.src), custom_call_target="tpu_custom_call" | custom-call | tf_op jit(solution)/shard_map/exchange/pallas_call | solution.py:212
  35.3 63.7 %solve.1.tiles = f32[384,8,128]{2,1,0:T(8,128)} custom-call(f32[16,6,4,8,128]{4,3,2,1,0:T(8,128)} %exchange.1.spectra, f32[128,128]{1,0:T(8,128)} %pad.4.penalty, f32[128,128]{1,0:T(8,128)} %constant.13.clone.laplace, f32[2,6]{1,0:T(2,128)} %constant.14.clone.table), custom_call_target="tpu_custom_call" | custom-call | tf_op jit(solution)/shard_map/solve/pallas_call | solution.py:489
  99.1 13.3 %unpack.1 = f32[11616,32]{1,0:T(8,128)} custom-call(f32[384,8,128]{2,1,0:T(8,128)} %solve.1.tiles), custom_call_target="tpu_custom_call" | custom-call | tf_op jit(solution)/shard_map/unpack/pallas_call | solution.py:533
  (2 shorter events, 0.0 us)

commit v2 on v1

v2 whole, which is shorter than its diff:
```python
import functools
import math

import jax
import jax.numpy as jnp
import ml_dtypes
import numpy as np
from jax import lax
from jax.experimental import pallas as pl
from jax.experimental.pallas import tpu as pltpu
from jax.sharding import PartitionSpec as P

ORDER = 10
NQ = ORDER + 1
NODES = NQ * NQ
PLANES = 512
MODES = 256
ITERS = 6
HELM_BASE = 1.0
SPAN_WAVE = 0.02
BOUND_RATIO = 25.0

COMPS = 3
PADDED = 128
OWNERS = 16
COLUMNS = 8
CHUNK = 64
HALF = ORDER // 2
UNROLL = True
MESH = pl.DeviceIdType.MESH
VMEM_LIMIT = 40 * 2**20


def legendre_pair(points, order):
    previous = points * 0.0 + 1.0
    current = points * 1.0
    for degree in range(2, order + 1):
        following = ((2 * degree - 1) * points * current - (degree - 1) * previous) / degree
        previous = current
        current = following
    return (current, previous)


def gll_tables(order):
    count = order + 1
    points = -np.cos(np.pi * np.arange(count) / order)
    for sweep in range(200):
        top_vals, below_vals = legendre_pair(points, order)
        points = points - (points * top_vals - below_vals) / (count * top_vals)
    legendre_vals, below_vals = legendre_pair(points, order)
    weights = 2.0 / (order * (order + 1) * legendre_vals**2)
    identity = np.eye(count)
    spacing = points[:, None] - points[None, :] + identity
    derivative = legendre_vals[:, None] / (legendre_vals[None, :] * spacing) * (1.0 - identity)
    corner = np.concatenate(
        [[-order * (order + 1) / 4.0], np.zeros(order - 1), [order * (order + 1) / 4.0]]
    )
    derivative = derivative + identity * corner[None, :]
    stiffness = derivative.T @ (weights[:, None] * derivative)
    weight_mat = identity * weights[None, :]
    laplace = np.kron(stiffness, weight_mat) + np.kron(weight_mat, stiffness)
    upper_bound = float(
        np.max(np.sum(np.abs(laplace), axis=1) / np.sum(laplace * np.eye(count * count), axis=1))
    )
    return weights, stiffness, derivative, upper_bound


WEIGHTS, STIFF, DERIV, TOP = gll_tables(ORDER)
SCALED = STIFF / WEIGHTS[:, None]


def chebyshev_table():
    low = TOP / BOUND_RATIO
    mid = (TOP + low) / 2.0
    half = (TOP - low) / 2.0
    table = [(0.0, 1.0 / mid)]
    recurrence = half / mid
    for step in range(ITERS - 1):
        following = 1.0 / (2.0 * mid / half - recurrence)
        table.append((following * recurrence, 2.0 * following / half))
        recurrence = following
    return np.asarray(table, np.float32).T.copy()


def dft_table():
    planes = np.arange(PLANES)
    modes = np.arange(MODES)
    angles = 2.0 * np.pi / PLANES * (modes[:, None] * planes[None, :] % PLANES)
    table = np.concatenate([np.cos(angles), -np.sin(angles)]) / math.sqrt(PLANES)
    high = table.astype(ml_dtypes.bfloat16)
    low = (table - high.astype(np.float64)).astype(ml_dtypes.bfloat16)
    return high, low


def lines(vals, matrix, sign):
    evens = [vals[k] + vals[ORDER - k] for k in range(HALF)]
    odds = [vals[k] - vals[ORDER - k] for k in range(HALF)]
    out = [None] * NQ
    for i in range(HALF):
        even = vals[HALF] * float(matrix[i, HALF])
        odd = None
        for k in range(HALF):
            even = even + evens[k] * float((matrix[i, k] + matrix[i, ORDER - k]) / 2)
            term = odds[k] * float((matrix[i, k] - matrix[i, ORDER - k]) / 2)
            odd = term if odd is None else odd + term
        out[i] = even + odd
        out[ORDER - i] = even - odd if sign > 0 else odd - even
    middle = vals[HALF] * float(matrix[HALF, HALF]) if sign > 0 else None
    for k in range(HALF):
        term = (evens if sign > 0 else odds)[k] * float(matrix[HALF, k])
        middle = term if middle is None else middle + term
    out[HALF] = middle
    return out


def roll(tile, by):
    return pltpu.roll(tile, by % 128, 1)


def join_rows(low, high):
    row = lax.broadcasted_iota(jnp.int32, (8, 128), 1) % 32
    above = jnp.where(row == 31, 0.0, roll(low, -1))
    below = jnp.where(row == 0, 0.0, roll(high, 1))
    return low + below, high + above


def step_kernel(
    vel,
    high,
    low,
    penalty,
    laplace,
    table,
    out,
    forcing,
    spectra,
    owned,
    res,
    direction,
    tmp,
    inverse,
    coeff,
    sent,
    got,
    pen_sent,
    pen_got,
    mode_send_sem,
    mode_recv_sem,
    local_sem,
    send_sem,
    recv_sem,
    pen_send_sem,
    pen_recv_sem,
):
    mode, column = lax.axis_index("mode"), lax.axis_index("mesh")
    has = (column > 0, column < COLUMNS - 1)
    partner = (jnp.maximum(column - 1, 0), jnp.minimum(column + 1, COLUMNS - 1))
    edge_rows = (0, ORDER)

    def chunk(c, owner):
        return pl.ds(pl.multiple_of((c * OWNERS + owner) * CHUNK, CHUNK), CHUNK)

    def mode_copy(c, offset):
        dest = lax.rem(mode + offset, OWNERS)
        return pltpu.make_async_remote_copy(
            src_ref=spectra.at[chunk(c, dest)],
            dst_ref=owned.at[chunk(c, mode)],
            send_sem=mode_send_sem.at[c, offset],
            recv_sem=mode_recv_sem.at[c, offset],
            device_id=(dest, column),
            device_id_type=MESH,
        )

    def local_copy(c):
        return pltpu.make_async_copy(
            spectra.at[chunk(c, mode)], owned.at[chunk(c, mode)], local_sem.at[c]
        )

    def face_copy(step, c, side):
        return pltpu.make_async_remote_copy(
            src_ref=sent.at[step, c, side],
            dst_ref=got.at[step, c, 1 - side],
            send_sem=send_sem.at[step, c, side],
            recv_sem=recv_sem.at[step, c, 1 - side],
            device_id=(mode, partner[side]),
            device_id_type=MESH,
        )

    def pen_copy(side):
        return pltpu.make_async_remote_copy(
            src_ref=pen_sent.at[side],
            dst_ref=pen_got.at[1 - side],
            send_sem=pen_send_sem.at[side],
            recv_sem=pen_recv_sem.at[1 - side],
            device_id=(mode, partner[side]),
            device_id_type=MESH,
        )

    def start_faces(step, c):
        for side in range(2):

            @pl.when(has[side])
            def _():
                face_copy(step, c, side).start()

    def wait_faces(step, c):
        for side in range(2):

            @pl.when(has[side])
            def _():
                face_copy(step, c, side).wait_send()
                face_copy(step, c, 1 - side).wait_recv()

    for side in range(2):

        @pl.when(jnp.logical_not(has[side]))
        def _():
            for step in range(ITERS):
                got[step, :, side] = jnp.zeros((COMPS, NQ, 8, 128), jnp.float32)

    barrier = pltpu.get_barrier_semaphore()
    for offset in range(1, OWNERS):
        dest = lax.rem(mode + offset, OWNERS)
        pl.semaphore_signal(barrier, inc=1, device_id=(dest, column), device_id_type=MESH)
    for side in range(2):

        @pl.when(has[side])
        def _():
            pl.semaphore_signal(
                barrier, inc=1, device_id=(mode, partner[side]), device_id_type=MESH
            )

    forcing[pl.ds(NODES * 8, (PADDED - NODES) * 8), :] = jnp.zeros(
        ((PADDED - NODES) * 8, 128), jnp.float32
    )
    for c in range(COMPS):

        def advect_first(b, _):
            grads = lines([vel[c * NODES + a * NQ + b] for a in range(NQ)], DERIV, -1)
            for a in range(NQ):
                tmp[a * NQ + b] = vel[a * NQ + b] * grads[a]
            return 0

        def advect_second(a, _):
            vals = [vel[c * NODES + a * NQ + b] for b in range(NQ)]
            grads = lines(vals, DERIV, -1)
            for b in range(NQ):
                node = a * NQ + b
                value = vals[b] - (tmp[node] + vel[NODES + node] * grads[b])
                forcing[pl.ds(pl.multiple_of(node * 8, 8), 8), :] = value
            return 0

        lax.fori_loop(0, NQ, advect_first, 0, unroll=UNROLL)
        lax.fori_loop(0, NQ, advect_second, 0, unroll=UNROLL)
        field = jnp.concatenate(
            [
                jnp.concatenate(
                    [forcing[pl.ds(t * 2 + y, PADDED, stride=8), :] for y in range(2)], axis=0
                )
                for t in range(4)
            ],
            axis=1,
        )
        upper = field.astype(jnp.bfloat16)
        lower = (field - upper.astype(jnp.float32)).astype(jnp.bfloat16)
        dot = functools.partial(
            lax.dot_general,
            dimension_numbers=(((1,), (1,)), ((), ())),
            preferred_element_type=jnp.float32,
        )
        modes = dot(high[...], upper) + (dot(high[...], lower) + dot(low[...], upper))
        for owner in range(OWNERS):
            for y in range(2):
                spectra[pl.ds((c * OWNERS + owner) * CHUNK + y * 32, 32), :] = modes[
                    owner * 32 : owner * 32 + 32, y * 128 : y * 128 + 128
                ]
        if c == 0:
            peers = OWNERS - 1 + has[0].astype(jnp.int32) + has[1].astype(jnp.int32)
            pl.semaphore_wait(barrier, peers)
        for offset in range(1, OWNERS):
            mode_copy(c, offset).start()
        local_copy(c).start()

    for side in range(2):
        pen_sent[side] = penalty[pl.ds(edge_rows[side] * NQ, 16), :]

        @pl.when(has[side])
        def _():
            pen_copy(side).start()

    block = lax.broadcasted_iota(jnp.int32, (8, 128), 1) // 32
    row = mode * 32 + block * 8 + lax.broadcasted_iota(jnp.int32, (8, 128), 0)
    wave = (row % MODES).astype(jnp.float32)
    helm = HELM_BASE + (SPAN_WAVE * wave) * (SPAN_WAVE * wave)

    def make_coeff(node, _):
        value = helm + penalty[pl.ds(node, 1), :]
        coeff[node] = value
        inverse[node] = value + laplace[pl.ds(node, 1), :]
        return 0

    lax.fori_loop(0, NODES, make_coeff, 0, unroll=11)
    for side in range(2):

        @pl.when(has[side])
        def _():
            pen_copy(side).wait_send()
            pen_copy(1 - side).wait_recv()
            for b in range(NQ):
                node = edge_rows[side] * NQ + b
                other = helm + pen_got[side, pl.ds(b, 1), :]
                inverse[node] += other + laplace[pl.ds(node, 1), :]

    def invert(a, _):
        vals = [inverse[a * NQ + b] for b in range(NQ)]
        vals[0], vals[ORDER] = join_rows(vals[0], vals[ORDER])
        for b in range(NQ):
            inverse[a * NQ + b] = 1.0 / vals[b]
        return 0

    lax.fori_loop(0, NQ, invert, 0, unroll=UNROLL)

    for c in range(COMPS):
        for offset in range(1, OWNERS):
            mode_copy(c, offset).wait_recv()
        local_copy(c).wait()

        def turn(r, _):
            first = c * OWNERS * CHUNK + r
            rows = [
                owned[pl.ds(first + (y * 32 + block * 8), 8, stride=32), :]
                for block in range(4)
                for y in range(0, 32, 8)
            ]
            tiles = jnp.concatenate(rows, axis=0).T
            for i in range(16):
                start = (c * PADDED + i * 8) * 8 + r
                res[pl.ds(start, 8, stride=8), :] = tiles[i * 8 : i * 8 + 8]
            return 0

        lax.fori_loop(0, 8, turn, 0, unroll=True)

        def join_rhs(a, _):
            node = c * PADDED + a * NQ
            low, high = join_rows(load(res, node), load(res, node + ORDER))
            store(res, node, low)
            store(res, node + ORDER, high)
            return 0

        lax.fori_loop(0, NQ, join_rhs, 0, unroll=UNROLL)
        zero = jnp.zeros((8, 128), jnp.float32)
        for side in range(2):
            for b in range(NQ):
                node = c * PADDED + edge_rows[side] * NQ + b
                sent[0, c, side, b] = -load(res, node)
                store(res, node, zero)
                direction[node] = zero
                out[node] = zero
        start_faces(0, c)

        def begin(i, _):
            node = NQ + i
            value = inverse[node] * load(res, c * PADDED + node) * table[1, 0]
            direction[c * PADDED + node] = value
            out[c * PADDED + node] = value
            return 0

        lax.fori_loop(0, NODES - 2 * NQ, begin, 0, unroll=11)

    def update(base, node, change, keep, gain):
        now = load(res, base + node) - change
        store(res, base + node, now)
        value = keep * direction[base + node] + gain * (inverse[node] * now)
        direction[base + node] = value
        out[base + node] += value

    def finish_faces(step, c):
        wait_faces(step, c)
        keep, gain = table[0, step], table[1, step]
        for side in range(2):
            for b in range(NQ):
                change = sent[step, c, side, b] + got[step, c, side, b]
                update(c * PADDED, edge_rows[side] * NQ + b, change, keep, gain)

    def along_second(base, a):
        terms = lines([direction[base + a * NQ + b] for b in range(NQ)], SCALED, 1)
        terms = [terms[b] + tmp[a * NQ + b] for b in range(NQ)]
        terms[0], terms[ORDER] = join_rows(terms[0], terms[ORDER])
        return terms

    def sweep(q, _):
        step, c = q // COMPS, q % COMPS
        base = c * PADDED
        finish_faces(step, c)

        def along_first(b, _):
            vals = [direction[base + a * NQ + b] for a in range(NQ)]
            terms = lines(vals, SCALED, 1)
            for a in range(NQ):
                tmp[a * NQ + b] = terms[a] + coeff[a * NQ + b] * vals[a]
            return 0

        lax.fori_loop(0, NQ, along_first, 0, unroll=UNROLL)
        for side in range(2):
            terms = along_second(base, edge_rows[side])
            for b in range(NQ):
                sent[step + 1, c, side, b] = terms[b]
        start_faces(step + 1, c)
        keep, gain = table[0, step + 1], table[1, step + 1]

        def interior(a, _):
            terms = along_second(base, a)
            for b in range(NQ):
                update(base, a * NQ + b, terms[b], keep, gain)
            return 0

        lax.fori_loop(1, ORDER, interior, 0, unroll=UNROLL)
        return 0

    lax.fori_loop(0, (ITERS - 1) * COMPS, sweep, 0)
    for c in range(COMPS):
        finish_faces(ITERS - 1, c)
        for offset in range(1, OWNERS):
            mode_copy(c, offset).wait_send()


def load(ref, node):
    return ref[pl.ds(pl.multiple_of(node * 8, 8), 8), :]


def store(ref, node, value):
    ref[pl.ds(pl.multiple_of(node * 8, 8), 8), :] = value


def run_step(velocity, penalty):
    tiles = velocity.reshape(COMPS * NODES, 2, 4, 128).transpose(0, 2, 1, 3)
    tiles = tiles.reshape(COMPS * NODES, 8, 128)
    high, low = dft_table()
    pen = jnp.tile(penalty.reshape(NODES, 32), (1, 4))
    pen = jnp.pad(pen, ((0, PADDED - NODES), (0, 0)))
    diag = np.diagonal(SCALED)
    laplace = np.zeros((PADDED, 128), np.float32)
    laplace[:NODES] = (diag[:, None] + diag[None, :]).reshape(NODES, 1)
    tile = (8, 128)
    vmem = pl.BlockSpec(memory_space=pltpu.VMEM)
    return pl.pallas_call(
        step_kernel,
        out_shape=jax.ShapeDtypeStruct((COMPS * PADDED,) + tile, jnp.float32),
        in_specs=[vmem] * 5 + [pl.BlockSpec(memory_space=pltpu.SMEM)],
        out_specs=vmem,
        scratch_shapes=[
            pltpu.VMEM((PADDED * 8, 128), jnp.float32),
            pltpu.VMEM((COMPS * OWNERS * CHUNK, 128), jnp.float32),
            pltpu.VMEM((COMPS * OWNERS * CHUNK, 128), jnp.float32),
            pltpu.VMEM((COMPS * PADDED * 8, 128), jnp.float32),
            pltpu.VMEM((COMPS * PADDED,) + tile, jnp.float32),
            pltpu.VMEM((PADDED,) + tile, jnp.float32),
            pltpu.VMEM((PADDED,) + tile, jnp.float32),
            pltpu.VMEM((PADDED,) + tile, jnp.float32),
            pltpu.VMEM((ITERS, COMPS, 2, NQ) + tile, jnp.float32),
            pltpu.VMEM((ITERS, COMPS, 2, NQ) + tile, jnp.float32),
            pltpu.VMEM((2, 16, 128), jnp.float32),
            pltpu.VMEM((2, 16, 128), jnp.float32),
            pltpu.SemaphoreType.DMA((COMPS, OWNERS)),
            pltpu.SemaphoreType.DMA((COMPS, OWNERS)),
            pltpu.SemaphoreType.DMA((COMPS,)),
            pltpu.SemaphoreType.DMA((ITERS, COMPS, 2)),
            pltpu.SemaphoreType.DMA((ITERS, COMPS, 2)),
            pltpu.SemaphoreType.DMA((2,)),
            pltpu.SemaphoreType.DMA((2,)),
        ],
        compiler_params=pltpu.CompilerParams(
            collective_id=0, has_side_effects=True, vmem_limit_bytes=VMEM_LIMIT
        ),
        name="step",
    )(tiles, jnp.asarray(high), jnp.asarray(low), pen, jnp.asarray(laplace), jnp.asarray(chebyshev_table()))


def unpack_kernel(tiles, out, rows, sem):
    size = 8 * COMPS * NODES
    copies = []
    for block in range(4):
        for c in range(COMPS):

            def one(node, _):
                tile = tiles[c * PADDED + node]
                if block:
                    tile = roll(tile, -32 * block)
                first = block * size + c * NODES + node
                rows[pl.ds(first, 8, stride=COMPS * NODES), :] = tile[:, :32]
                return 0

            lax.fori_loop(0, NODES, one, 0, unroll=11)
        part = pl.ds(block * size, size)
        copies.append(pltpu.make_async_copy(rows.at[part], out.at[part], sem.at[block]))
        copies[-1].start()
    for copy in copies:
        copy.wait()


def unpack_output(tiles):
    shape = (32 * COMPS * NODES, 32)
    out = pl.pallas_call(
        unpack_kernel,
        out_shape=jax.ShapeDtypeStruct(shape, jnp.float32),
        in_specs=[pl.BlockSpec(memory_space=pltpu.VMEM)],
        out_specs=pl.BlockSpec(memory_space=pl.ANY),
        scratch_shapes=[pltpu.VMEM(shape, jnp.float32), pltpu.SemaphoreType.DMA((4,))],
        compiler_params=pltpu.CompilerParams(vmem_limit_bytes=VMEM_LIMIT),
        name="unpack",
    )(tiles)
    return out.reshape(32, COMPS, NQ, NQ, 1, 32)


def per_device(velocity, penalty):
    return unpack_output(run_step(velocity, penalty))


def solution(mesh):
    return jax.shard_map(
        per_device,
        mesh=mesh,
        in_specs=(P(None, None, None, "mesh", "mode", None), P(None, None, "mesh", None)),
        out_specs=P("mode", None, None, None, "mesh", None),
        check_vma=False,
    )
```

time: 114 us -> 73.7 us (0.65); the launches traced: 112 us -> 73.3 us
  Pallas kernels: 110 us -> 67.1 us
  local copies, waits for them, and re-layouts: 1.9 us -> 5.17 us
    pallas_call x4 -> x2, Pallas kernels: 110 us -> 67.1 us  [the longest x1 57.9 us: run_step(): pl.pallas_call(step_kernel, out_shape=jax.ShapeDtypeStruct((COMPS * PADDE...]
    unnamed x1 -> x10, local copies, waits for them, and re-layouts: 1.02 us -> 4.98 us
where the time goes in v2:
time: 73.7 us; the launch traced here: 73.3 us
  Pallas kernels  67.1 us (91%)
  local copies, waits for them, and re-layouts  5.17 us (7%)
  other arithmetic  0.99 us (1%)
    pallas_call x1, Pallas kernels, run_step(): pl.pallas_call(step_kernel, out_shape=jax.ShapeDtypeStruct((COMPS * PADDE...  57.9 us
    pallas_call x1, Pallas kernels, unpack_output(): pl.pallas_call(unpack_kernel, out_shape=jax.ShapeDtypeStruct(shape, jnp.f...  9.21 us
    unnamed x10, local copies, waits for them, and re-layouts  4.98 us

profile of v2, /device:TPU:96, one launch (start us, length us, event | category | flops | bytes accessed | tf_op | source)
XLA Modules:
  0.0 73.3 jit_solution(11068870677391895293)
XLA Ops:
  0.0 1.0 %reduce = f32[11,11,32]{2,1,0:T(8,128)S(1)} reduce(f32[11,11,1,32]{3,2,1,0:T(1,128)} %param.7, f32[]{:T(128)} %constant.19), dimensions={2}, to_apply=%param.7.reduce_sub_computation | reduce | bytes 30980 | tf_op args[1]
  1.0 0.1 copy.10
  1.1 0.1 copy.11
  1.2 0.0 copy-start
  1.2 1.4 %copy-done = f32[3,11,11,1,2,512]{5,4,3,2,1,0:T(2,128)S(1)} copy-done((f32[3,11,11,1,2,512]{5,4,3,2,1,0:T(2,128)S(1)}, f32[3,11,11,1,2,512]{5,4,3,2,1,0:T(2,128)}, u32[]{:S(2)}) %copy-start) | copy-done | bytes 1486872
  2.6 0.0 copy-start.1
  2.6 1.0 %copy-done.1 = bf16[512,512]{1,0:T(8,128)(2,1)S(1)} copy-done((bf16[512,512]{1,0:T(8,128)(2,1)S(1)}, bf16[512,512]{1,0:T(8,128)(2,1)}, u32[]{:S(2)}) %copy-start.1) | copy-done | bytes 524312
  3.6 0.0 copy-start.2
  3.6 1.0 %copy-done.2 = bf16[512,512]{1,0:T(8,128)(2,1)S(1)} copy-done((bf16[512,512]{1,0:T(8,128)(2,1)S(1)}, bf16[512,512]{1,0:T(8,128)(2,1)}, u32[]{:S(2)}) %copy-start.2) | copy-done | bytes 524312
  4.7 0.0 copy-start.3
  4.7 0.8 %copy-done.3 = f32[128,128]{1,0:T(8,128)S(1)} copy-done((f32[128,128]{1,0:T(8,128)S(1)}, f32[128,128]{1,0:T(8,128)}, u32[]{:S(2)}) %copy-start.3) | copy-done | bytes 65560
  5.5 0.0 copy-start.4
  5.5 0.7 copy-done.4
  6.2 57.9 %step.1.tiles = f32[384,8,128]{2,1,0:T(8,128)S(1)} custom-call(f32[363,8,128]{2,1,0:T(8,128)S(1)} %bitcast.7, bf16[512,512]{1,0:T(8,128)(2,1)S(1)} %copy-done.2, bf16[512,512]{1,0:T(8,128)(2,1)S(1)} %copy-done.1, f32[128,128]{1,0:T(8,128)S(1)} %pad.4.penalty, f32[128,128]{1,0:T(8,128)S(1)} %copy-done.3, f32[2,6]{1,0:T(2,128)S(1)} %copy-done.4), custom_call_target="tpu_custom_call" | custom-call | tf_op jit(solution)/shard_map/step/pallas_call | solution.py:446
  64.1 9.2 %unpack.1 = f32[11616,32]{1,0:T(8,128)} custom-call(f32[384,8,128]{2,1,0:T(8,128)S(1)} %step.1.tiles), custom_call_target="tpu_custom_call" | custom-call | tf_op jit(solution)/shard_map/unpack/pallas_call | solution.py:503
  (3 shorter events, 0.0 us)
Async XLA Ops:
  1.2 1.4 %copy-start = (f32[3,11,11,1,2,512]{5,4,3,2,1,0:T(2,128)S(1)}, f32[3,11,11,1,2,512]{5,4,3,2,1,0:T(2,128)}, u32[]{:S(2)}) copy-start(f32[3,11,11,1,2,512]{5,4,3,2,1,0:T(2,128)} %param.6) | copy-start | bytes 4460548
  2.6 1.0 %copy-start.1 = (bf16[512,512]{1,0:T(8,128)(2,1)S(1)}, bf16[512,512]{1,0:T(8,128)(2,1)}, u32[]{:S(2)}) copy-start(bf16[512,512]{1,0:T(8,128)(2,1)} %constant.12.clone.low) | copy-start | bytes 1572868
  3.6 1.0 %copy-start.2 = (bf16[512,512]{1,0:T(8,128)(2,1)S(1)}, bf16[512,512]{1,0:T(8,128)(2,1)}, u32[]{:S(2)}) copy-start(bf16[512,512]{1,0:T(8,128)(2,1)} %constant.11.clone.high) | copy-start | bytes 1572868
  4.7 0.8 %copy-start.3 = (f32[128,128]{1,0:T(8,128)S(1)}, f32[128,128]{1,0:T(8,128)}, u32[]{:S(2)}) copy-start(f32[128,128]{1,0:T(8,128)} %constant.13.clone.laplace) | copy-start | bytes 196612
  5.5 0.7 copy-start.4

commit v3 on v2

--- a/solution.py
+++ b/solution.py
@@ -28,7 +28,7 @@
 HALF = ORDER // 2
 UNROLL = True
 MESH = pl.DeviceIdType.MESH
-VMEM_LIMIT = 40 * 2**20
+VMEM_LIMIT = 60 * 2**20
 
 
 def legendre_pair(points, order):
@@ -79,7 +79,18 @@
         following = 1.0 / (2.0 * mid / half - recurrence)
         table.append((following * recurrence, 2.0 * following / half))
         recurrence = following
-    return np.asarray(table, np.float32).T.copy()
+    return table
+
+
+CHEBYSHEV = chebyshev_table()
+
+
+def coefficients(step):
+    keep, gain = CHEBYSHEV[0]
+    for i in range(1, ITERS):
+        keep = jnp.where(step == i, CHEBYSHEV[i][0], keep)
+        gain = jnp.where(step == i, CHEBYSHEV[i][1], gain)
+    return keep, gain
 
 
 def dft_table():
@@ -113,6 +124,17 @@
     return out
 
 
+def edge_lines(vals):
+    even = vals[HALF] * float(SCALED[0, HALF])
+    odd = None
+    for k in range(1, HALF):
+        near, far = float(SCALED[0, k]), float(SCALED[0, ORDER - k])
+        even = even + (vals[k] + vals[ORDER - k]) * ((near + far) / 2)
+        term = (vals[k] - vals[ORDER - k]) * ((near - far) / 2)
+        odd = term if odd is None else odd + term
+    return even + odd, even - odd
+
+
 def roll(tile, by):
     return pltpu.roll(tile, by % 128, 1)
 
@@ -125,13 +147,18 @@
 
 
 def step_kernel(
+    vel_in,
+    high_in,
+    low_in,
+    pen_in,
+    result,
+    out,
     vel,
     high,
     low,
+    pen_rows,
     penalty,
-    laplace,
-    table,
-    out,
+    edges,
     forcing,
     spectra,
     owned,
@@ -151,11 +178,25 @@
     recv_sem,
     pen_send_sem,
     pen_recv_sem,
+    load_sem,
+    out_sem,
 ):
     mode, column = lax.axis_index("mode"), lax.axis_index("mesh")
     has = (column > 0, column < COLUMNS - 1)
     partner = (jnp.maximum(column - 1, 0), jnp.minimum(column + 1, COLUMNS - 1))
     edge_rows = (0, ORDER)
+
+    loads = [
+        pltpu.make_async_copy(
+            vel_in.at[pl.ds(c * NODES, NODES)], vel.at[pl.ds(c * NODES, NODES)], load_sem.at[c]
+        )
+        for c in range(COMPS)
+    ]
+    load_high = pltpu.make_async_copy(high_in, high, load_sem.at[3])
+    load_low = pltpu.make_async_copy(low_in, low, load_sem.at[4])
+    load_pen = pltpu.make_async_copy(pen_in, pen_rows, load_sem.at[5])
+    for copy in [loads[0], loads[1], load_high, load_low, loads[2], load_pen]:
+        copy.start()
 
     def chunk(c, owner):
         return pl.ds(pl.multiple_of((c * OWNERS + owner) * CHUNK, CHUNK), CHUNK)
@@ -208,7 +249,6 @@
 
             @pl.when(has[side])
             def _():
-                face_copy(step, c, side).wait_send()
                 face_copy(step, c, 1 - side).wait_recv()
 
     for side in range(2):
@@ -230,10 +270,12 @@
                 barrier, inc=1, device_id=(mode, partner[side]), device_id_type=MESH
             )
 
-    forcing[pl.ds(NODES * 8, (PADDED - NODES) * 8), :] = jnp.zeros(
-        ((PADDED - NODES) * 8, 128), jnp.float32
-    )
-    for c in range(COMPS):
+    def node_rows(c, node):
+        return pl.ds(pl.multiple_of((c * PADDED + node) * 8, 8), 8)
+
+    def advect(c):
+        pad = pl.ds((c * PADDED + NODES) * 8, (PADDED - NODES) * 8)
+        forcing[pad, :] = jnp.zeros(((PADDED - NODES) * 8, 128), jnp.float32)
 
         def advect_first(b, _):
             grads = lines([vel[c * NODES + a * NQ + b] for a in range(NQ)], DERIV, -1)
@@ -247,15 +289,33 @@
             for b in range(NQ):
                 node = a * NQ + b
                 value = vals[b] - (tmp[node] + vel[NODES + node] * grads[b])
-                forcing[pl.ds(pl.multiple_of(node * 8, 8), 8), :] = value
+                forcing[node_rows(c, node), :] = value
             return 0
 
         lax.fori_loop(0, NQ, advect_first, 0, unroll=UNROLL)
         lax.fori_loop(0, NQ, advect_second, 0, unroll=UNROLL)
+
+    def send_forcing_faces(c):
+        for side in range(2):
+            for b in range(NQ):
+                sent[0, c, side, b] = forcing[node_rows(c, edge_rows[side] * NQ + b), :]
+        start_faces(0, c)
+
+    def add_forcing_faces(c):
+        wait_faces(0, c)
+        for side in range(2):
+            for b in range(NQ):
+                forcing[node_rows(c, edge_rows[side] * NQ + b), :] += got[0, c, side, b]
+
+    def transform(c):
         field = jnp.concatenate(
             [
                 jnp.concatenate(
-                    [forcing[pl.ds(t * 2 + y, PADDED, stride=8), :] for y in range(2)], axis=0
+                    [
+                        forcing[pl.ds(c * PADDED * 8 + t * 2 + y, PADDED, stride=8), :]
+                        for y in range(2)
+                    ],
+                    axis=0,
                 )
                 for t in range(4)
             ],
@@ -274,58 +334,77 @@
                 spectra[pl.ds((c * OWNERS + owner) * CHUNK + y * 32, 32), :] = modes[
                     owner * 32 : owner * 32 + 32, y * 128 : y * 128 + 128
                 ]
-        if c == 0:
-            peers = OWNERS - 1 + has[0].astype(jnp.int32) + has[1].astype(jnp.int32)
-            pl.semaphore_wait(barrier, peers)
         for offset in range(1, OWNERS):
             mode_copy(c, offset).start()
         local_copy(c).start()
 
+    loads[0].wait()
+    loads[1].wait()
+    advect(0)
+    advect(1)
+    peers = OWNERS - 1 + has[0].astype(jnp.int32) + has[1].astype(jnp.int32)
+    pl.semaphore_wait(barrier, peers)
+    send_forcing_faces(1)
+    load_high.wait()
+    load_low.wait()
+    transform(0)
+    loads[2].wait()
+    advect(2)
+    send_forcing_faces(2)
+
+    load_pen.wait()
+    for node in range(NODES):
+        line = pen_rows[node]
+        penalty[pl.ds(node, 1), :] = jnp.concatenate([line] * 4, axis=1)
     for side in range(2):
-        pen_sent[side] = penalty[pl.ds(edge_rows[side] * NQ, 16), :]
+        for b in range(NQ):
+            node = edge_rows[side] * NQ + b
+            pen_sent[side, pl.ds(b, 1), :] = penalty[pl.ds(node, 1), :]
+        pen_sent[side, pl.ds(NQ, 16 - NQ), :] = jnp.zeros((16 - NQ, 128), jnp.float32)
 
         @pl.when(has[side])
         def _():
             pen_copy(side).start()
+
+    add_forcing_faces(1)
+    transform(1)
 
     block = lax.broadcasted_iota(jnp.int32, (8, 128), 1) // 32
     row = mode * 32 + block * 8 + lax.broadcasted_iota(jnp.int32, (8, 128), 0)
     wave = (row % MODES).astype(jnp.float32)
     helm = HELM_BASE + (SPAN_WAVE * wave) * (SPAN_WAVE * wave)
 
-    def make_coeff(node, _):
-        value = helm + penalty[pl.ds(node, 1), :]
-        coeff[node] = value
-        inverse[node] = value + laplace[pl.ds(node, 1), :]
-        return 0
-
-    lax.fori_loop(0, NODES, make_coeff, 0, unroll=11)
+    diag = [float(SCALED[i, i]) for i in range(NQ)]
+    for a in range(NQ):
+        for b in range(NQ):
+            value = helm + penalty[pl.ds(a * NQ + b, 1), :]
+            coeff[a * NQ + b] = value
+            inverse[a * NQ + b] = value + (diag[a] + diag[b])
+
+    add_forcing_faces(2)
+    transform(2)
+
     for side in range(2):
 
         @pl.when(has[side])
         def _():
-            pen_copy(side).wait_send()
             pen_copy(1 - side).wait_recv()
             for b in range(NQ):
                 node = edge_rows[side] * NQ + b
                 other = helm + pen_got[side, pl.ds(b, 1), :]
-                inverse[node] += other + laplace[pl.ds(node, 1), :]
-
-    def invert(a, _):
+                inverse[node] += other + (diag[edge_rows[side]] + diag[b])
+
+    for a in range(NQ):
         vals = [inverse[a * NQ + b] for b in range(NQ)]
         vals[0], vals[ORDER] = join_rows(vals[0], vals[ORDER])
         for b in range(NQ):
             inverse[a * NQ + b] = 1.0 / vals[b]
-        return 0
-
-    lax.fori_loop(0, NQ, invert, 0, unroll=UNROLL)
-
-    for c in range(COMPS):
+
+    def begin(c):
         for offset in range(1, OWNERS):
             mode_copy(c, offset).wait_recv()
         local_copy(c).wait()
-
-        def turn(r, _):
+        for r in range(8):
             first = c * OWNERS * CHUNK + r
             rows = [
                 owned[pl.ds(first + (y * 32 + block * 8), 8, stride=32), :]
@@ -336,36 +415,28 @@
             for i in range(16):
                 start = (c * PADDED + i * 8) * 8 + r
                 res[pl.ds(start, 8, stride=8), :] = tiles[i * 8 : i * 8 + 8]
-            return 0
-
-        lax.fori_loop(0, 8, turn, 0, unroll=True)
-
-        def join_rhs(a, _):
+        for a in range(NQ):
             node = c * PADDED + a * NQ
             low, high = join_rows(load(res, node), load(res, node + ORDER))
             store(res, node, low)
             store(res, node + ORDER, high)
-            return 0
-
-        lax.fori_loop(0, NQ, join_rhs, 0, unroll=UNROLL)
-        zero = jnp.zeros((8, 128), jnp.float32)
-        for side in range(2):
-            for b in range(NQ):
-                node = c * PADDED + edge_rows[side] * NQ + b
-                sent[0, c, side, b] = -load(res, node)
-                store(res, node, zero)
-                direction[node] = zero
-                out[node] = zero
-        start_faces(0, c)
-
-        def begin(i, _):
-            node = NQ + i
-            value = inverse[node] * load(res, c * PADDED + node) * table[1, 0]
-            direction[c * PADDED + node] = value
-            out[c * PADDED + node] = value
-            return 0
-
-        lax.fori_loop(0, NODES - 2 * NQ, begin, 0, unroll=11)
+        nodes = range(NODES)
+        if c == 0:
+            zero = jnp.zeros((8, 128), jnp.float32)
+            for side in range(2):
+                for b in range(NQ):
+                    node = edge_rows[side] * NQ + b
+                    sent[0, c, side, b] = -load(res, node)
+                    store(res, node, zero)
+                    direction[node] = zero
+                    out[node] = zero
+            start_faces(0, c)
+            nodes = range(NQ, NODES - NQ)
+        for i in nodes:
+            value = inverse[i] * load(res, c * PADDED + i) * CHEBYSHEV[0][1]
+            direction[c * PADDED + i] = value
+            out[c * PADDED + i] = value
+        prepare_edges(c)
 
     def update(base, node, change, keep, gain):
         now = load(res, base + node) - change
@@ -376,52 +447,90 @@
 
     def finish_faces(step, c):
         wait_faces(step, c)
-        keep, gain = table[0, step], table[1, step]
+        keep, gain = coefficients(step)
         for side in range(2):
             for b in range(NQ):
                 change = sent[step, c, side, b] + got[step, c, side, b]
                 update(c * PADDED, edge_rows[side] * NQ + b, change, keep, gain)
 
-    def along_second(base, a):
-        terms = lines([direction[base + a * NQ + b] for b in range(NQ)], SCALED, 1)
-        terms = [terms[b] + tmp[a * NQ + b] for b in range(NQ)]
-        terms[0], terms[ORDER] = join_rows(terms[0], terms[ORDER])
-        return terms
-
-    def sweep(q, _):
-        step, c = q // COMPS, q % COMPS
+    def prepare_edges(c):
+        for b in range(NQ):
+            vals = [direction[c * PADDED + a * NQ + b] for a in range(1, ORDER)]
+            edges[c * 2 * NQ + b], edges[c * 2 * NQ + NQ + b] = edge_lines([None] + vals + [None])
+
+    def send_edges(step, c):
         base = c * PADDED
-        finish_faces(step, c)
+        own, across = float(SCALED[0, 0]), float(SCALED[0, ORDER])
+        for side in range(2):
+            node = edge_rows[side] * NQ
+            other = edge_rows[1 - side] * NQ
+            vals = [direction[base + node + b] for b in range(NQ)]
+            terms = lines(vals, SCALED, 1)
+            for b in range(NQ):
+                first = edges[c * 2 * NQ + side * NQ + b] + direction[base + other + b] * across
+                terms[b] = terms[b] + first + vals[b] * (coeff[node + b] + own)
+            terms[0], terms[ORDER] = join_rows(terms[0], terms[ORDER])
+            for b in range(NQ):
+                sent[step, c, side, b] = terms[b]
+        start_faces(step, c)
+
+    def interior(step, c):
+        base = c * PADDED
+        keep, gain = coefficients(step)
 
         def along_first(b, _):
             vals = [direction[base + a * NQ + b] for a in range(NQ)]
             terms = lines(vals, SCALED, 1)
-            for a in range(NQ):
+            for a in range(1, ORDER):
                 tmp[a * NQ + b] = terms[a] + coeff[a * NQ + b] * vals[a]
             return 0
 
-        lax.fori_loop(0, NQ, along_first, 0, unroll=UNROLL)
-        for side in range(2):
-            terms = along_second(base, edge_rows[side])
-            for b in range(NQ):
-                sent[step + 1, c, side, b] = terms[b]
-        start_faces(step + 1, c)
-        keep, gain = table[0, step + 1], table[1, step + 1]
-
-        def interior(a, _):
-            terms = along_second(base, a)
+        def along_second(a, _):
+            terms = lines([direction[base + a * NQ + b] for b in range(NQ)], SCALED, 1)
+            terms = [terms[b] + tmp[a * NQ + b] for b in range(NQ)]
+            terms[0], terms[ORDER] = join_rows(terms[0], terms[ORDER])
             for b in range(NQ):
                 update(base, a * NQ + b, terms[b], keep, gain)
             return 0
 
-        lax.fori_loop(1, ORDER, interior, 0, unroll=UNROLL)
+        lax.fori_loop(0, NQ, along_first, 0, unroll=UNROLL)
+        lax.fori_loop(1, ORDER, along_second, 0, unroll=UNROLL)
+        prepare_edges(c)
+
+    def sweep(q, _):
+        step, c = q // COMPS, q % COMPS
+        finish_faces(step, c)
+        send_edges(step + 1, c)
+        interior(step + 1, c)
         return 0
 
-    lax.fori_loop(0, (ITERS - 1) * COMPS, sweep, 0)
+    begin(0)
+    finish_faces(0, 0)
+    for c in range(COMPS):
+        send_edges(1, c)
+        interior(1, c)
+        if c + 1 < COMPS:
+            begin(c + 1)
+    lax.fori_loop(COMPS, (ITERS - 1) * COMPS, sweep, 0)
+    saves = []
     for c in range(COMPS):
         finish_faces(ITERS - 1, c)
+        part = pl.ds(c * PADDED, NODES)
+        saves.append(pltpu.make_async_copy(out.at[part], result.at[part], out_sem.at[c]))
+        saves[-1].start()
+
+    for c in range(COMPS):
+        saves[c].wait()
         for offset in range(1, OWNERS):
             mode_copy(c, offset).wait_send()
+    for side in range(2):
+
+        @pl.when(has[side])
+        def _():
+            pen_copy(side).wait_send()
+            for step in range(ITERS):
+                for c in range(COMPS):
+                    face_copy(step, c, side).wait_send()
 
 
 def load(ref, node):
@@ -436,20 +545,22 @@
     tiles = velocity.reshape(COMPS * NODES, 2, 4, 128).transpose(0, 2, 1, 3)
     tiles = tiles.reshape(COMPS * NODES, 8, 128)
     high, low = dft_table()
-    pen = jnp.tile(penalty.reshape(NODES, 32), (1, 4))
-    pen = jnp.pad(pen, ((0, PADDED - NODES), (0, 0)))
-    diag = np.diagonal(SCALED)
-    laplace = np.zeros((PADDED, 128), np.float32)
-    laplace[:NODES] = (diag[:, None] + diag[None, :]).reshape(NODES, 1)
+    pen = penalty.reshape(NODES, 1, 32)
     tile = (8, 128)
-    vmem = pl.BlockSpec(memory_space=pltpu.VMEM)
     return pl.pallas_call(
         step_kernel,
         out_shape=jax.ShapeDtypeStruct((COMPS * PADDED,) + tile, jnp.float32),
-        in_specs=[vmem] * 5 + [pl.BlockSpec(memory_space=pltpu.SMEM)],
-        out_specs=vmem,
+        in_specs=[pl.BlockSpec(memory_space=pltpu.HBM)] * 4,
+        out_specs=pl.BlockSpec(memory_space=pltpu.HBM),
         scratch_shapes=[
-            pltpu.VMEM((PADDED * 8, 128), jnp.float32),
+            pltpu.VMEM((COMPS * PADDED,) + tile, jnp.float32),
+            pltpu.VMEM((COMPS * NODES,) + tile, jnp.float32),
+            pltpu.VMEM((PLANES, PLANES), jnp.bfloat16),
+            pltpu.VMEM((PLANES, PLANES), jnp.bfloat16),
+            pltpu.VMEM((NODES, 1, 32), jnp.float32),
+            pltpu.VMEM((PADDED, 128), jnp.float32),
+            pltpu.VMEM((COMPS * 2 * NQ,) + tile, jnp.float32),
+            pltpu.VMEM((COMPS * PADDED * 8, 128), jnp.float32),
             pltpu.VMEM((COMPS * OWNERS * CHUNK, 128), jnp.float32),
             pltpu.VMEM((COMPS * OWNERS * CHUNK, 128), jnp.float32),
             pltpu.VMEM((COMPS * PADDED * 8, 128), jnp.float32),
@@ -468,29 +579,34 @@
             pltpu.SemaphoreType.DMA((ITERS, COMPS, 2)),
             pltpu.SemaphoreType.DMA((2,)),
             pltpu.SemaphoreType.DMA((2,)),
+            pltpu.SemaphoreType.DMA((6,)),
+            pltpu.SemaphoreType.DMA((COMPS,)),
         ],
         compiler_params=pltpu.CompilerParams(
             collective_id=0, has_side_effects=True, vmem_limit_bytes=VMEM_LIMIT
         ),
         name="step",
-    )(tiles, jnp.asarray(high), jnp.asarray(low), pen, jnp.asarray(laplace), jnp.asarray(chebyshev_table()))
-
-
-def unpack_kernel(tiles, out, rows, sem):
+    )(tiles, jnp.asarray(high), jnp.asarray(low), pen)
+
+
+def unpack_kernel(tiles_in, out, tiles, rows, load_sem, sem):
+    loads = []
+    for c in range(COMPS):
+        part = pl.ds(c * PADDED, NODES)
+        loads.append(pltpu.make_async_copy(tiles_in.at[part], tiles.at[part], load_sem.at[c]))
+        loads[-1].start()
     size = 8 * COMPS * NODES
     copies = []
     for block in range(4):
         for c in range(COMPS):
-
-            def one(node, _):
+            if block == 0:
+                loads[c].wait()
+            for node in range(NODES):
                 tile = tiles[c * PADDED + node]
                 if block:
                     tile = roll(tile, -32 * block)
                 first = block * size + c * NODES + node
                 rows[pl.ds(first, 8, stride=COMPS * NODES), :] = tile[:, :32]
-                return 0
-
-            lax.fori_loop(0, NODES, one, 0, unroll=11)
         part = pl.ds(block * size, size)
         copies.append(pltpu.make_async_copy(rows.at[part], out.at[part], sem.at[block]))
         copies[-1].start()
@@ -503,9 +619,14 @@
     out = pl.pallas_call(
         unpack_kernel,
         out_shape=jax.ShapeDtypeStruct(shape, jnp.float32),
-        in_specs=[pl.BlockSpec(memory_space=pltpu.VMEM)],
-        out_specs=pl.BlockSpec(memory_space=pl.ANY),
-        scratch_shapes=[pltpu.VMEM(shape, jnp.float32), pltpu.SemaphoreType.DMA((4,))],
+        in_specs=[pl.BlockSpec(memory_space=pltpu.HBM)],
+        out_specs=pl.BlockSpec(memory_space=pltpu.HBM),
+        scratch_shapes=[
+            pltpu.VMEM(tiles.shape, jnp.float32),
+            pltpu.VMEM(shape, jnp.float32),
+            pltpu.SemaphoreType.DMA((COMPS,)),
+            pltpu.SemaphoreType.DMA((4,)),
+        ],
         compiler_params=pltpu.CompilerParams(vmem_limit_bytes=VMEM_LIMIT),
         name="unpack",
     )(tiles)

time: 73.7 us -> 58.9 us (0.80)
  Pallas kernels: 67.1 us -> 58.4 us
  local copies, waits for them, and re-layouts: 5.17 us -> 0 us
  other arithmetic: 0.99 us -> 0 us
    pallas_call x1, Pallas kernels: 9.21 us -> 4.01 us  [unpack_output(): pl.pallas_call(unpack_kernel, out_shape=jax.ShapeDtypeStruct(shape, jnp.f...]
    unnamed x10 -> x0, local copies, waits for them, and re-layouts: 4.98 us -> none
    pallas_call x1, Pallas kernels: 57.9 us -> 54.3 us  [run_step(): pl.pallas_call(step_kernel, out_shape=jax.ShapeDtypeStruct((COMPS * PADDE...]
    unnamed x1 -> x0, other arithmetic: 0.99 us -> none
where the time goes in v3:
time: 58.9 us; the launch traced here: 58.4 us
  Pallas kernels  58.4 us (99%)
    pallas_call x1, Pallas kernels, run_step(): pl.pallas_call(step_kernel, out_shape=jax.ShapeDtypeStruct((COMPS * PADDE...  54.3 us
    pallas_call x1, Pallas kernels, unpack_output(): pl.pallas_call(unpack_kernel, out_shape=jax.ShapeDtypeStruct(shape, jnp.f...  4.01 us

profile of v3, /device:TPU:96, one launch (start us, length us, event | category | flops | bytes accessed | tf_op | source)
XLA Modules:
  0.0 58.4 jit_solution(17913741301890676596)
XLA Ops:
  0.0 54.3 %step.1.tiles_in = f32[384,8,128]{2,1,0:T(8,128)} custom-call(f32[363,8,128]{2,1,0:T(8,128)} %bitcast.7, bf16[512,512]{1,0:T(8,128)(2,1)} %constant.4.clone.high_in, bf16[512,512]{1,0:T(8,128)(2,1)} %constant.5.clone.low_in, f32[121,1,32]{2,1,0:T(1,128)} %bitcast.8), custom_call_target="tpu_custom_call" | custom-call | tf_op jit(solution)/shard_map/step/pallas_call | solution.py:550
  54.3 4.0 %unpack.1 = f32[11616,32]{1,0:T(8,128)} custom-call(f32[384,8,128]{2,1,0:T(8,128)} %step.1.tiles_in), custom_call_target="tpu_custom_call" | custom-call | tf_op jit(solution)/shard_map/unpack/pallas_call | solution.py:619

commit v4 on v3

--- a/solution.py
+++ b/solution.py
@@ -159,6 +159,7 @@
     pen_rows,
     penalty,
     edges,
+    faces,
     forcing,
     spectra,
     owned,
@@ -182,8 +183,17 @@
     out_sem,
 ):
     mode, column = lax.axis_index("mode"), lax.axis_index("mesh")
-    has = (column > 0, column < COLUMNS - 1)
+
+    def neighbour(side):
+        return column + 2 * side - 1
+
+    def has_neighbour(side):
+        return (neighbour(side) >= 0) & (neighbour(side) < COLUMNS)
+
+    has = (has_neighbour(0), has_neighbour(1))
     partner = (jnp.maximum(column - 1, 0), jnp.minimum(column + 1, COLUMNS - 1))
+    inner = jnp.where(column < COLUMNS // 2, 1, 0)
+    outer = 1 - inner
     edge_rows = (0, ORDER)
 
     loads = [
@@ -223,7 +233,7 @@
             dst_ref=got.at[step, c, 1 - side],
             send_sem=send_sem.at[step, c, side],
             recv_sem=recv_sem.at[step, c, 1 - side],
-            device_id=(mode, partner[side]),
+            device_id=(mode, jnp.clip(neighbour(side), 0, COLUMNS - 1)),
             device_id_type=MESH,
         )
 
@@ -237,19 +247,23 @@
             device_id_type=MESH,
         )
 
+    def start_face(step, c, side):
+        @pl.when(has_neighbour(side))
+        def _():
+            face_copy(step, c, side).start()
+
+    def wait_face(step, c, side):
+        @pl.when(has_neighbour(side))
+        def _():
+            face_copy(step, c, 1 - side).wait_recv()
+
     def start_faces(step, c):
         for side in range(2):
-
-            @pl.when(has[side])
-            def _():
-                face_copy(step, c, side).start()
+            start_face(step, c, side)
 
     def wait_faces(step, c):
         for side in range(2):
-
-            @pl.when(has[side])
-            def _():
-                face_copy(step, c, 1 - side).wait_recv()
+            wait_face(step, c, side)
 
     for side in range(2):
 
@@ -385,6 +399,8 @@
     transform(2)
 
     for side in range(2):
+        for b in range(NQ):
+            faces[side * NQ + b] = coeff[edge_rows[side] * NQ + b] + diag[0]
 
         @pl.when(has[side])
         def _():
@@ -393,6 +409,7 @@
                 node = edge_rows[side] * NQ + b
                 other = helm + pen_got[side, pl.ds(b, 1), :]
                 inverse[node] += other + (diag[edge_rows[side]] + diag[b])
+                faces[side * NQ + b] += other + diag[0]
 
     for a in range(NQ):
         vals = [inverse[a * NQ + b] for b in range(NQ)]
@@ -445,34 +462,37 @@
         direction[base + node] = value
         out[base + node] += value
 
-    def finish_faces(step, c):
-        wait_faces(step, c)
-        keep, gain = coefficients(step)
+    def finish_rhs(c):
+        wait_faces(0, c)
         for side in range(2):
             for b in range(NQ):
-                change = sent[step, c, side, b] + got[step, c, side, b]
-                update(c * PADDED, edge_rows[side] * NQ + b, change, keep, gain)
+                change = sent[0, c, side, b] + got[0, c, side, b]
+                update(c * PADDED, edge_rows[side] * NQ + b, change, *CHEBYSHEV[0])
+
+    def finish_face(step, c, side):
+        keep, gain = coefficients(step)
+        owners = 1.0 + has_neighbour(side).astype(jnp.float32)
+        vals = [direction[c * PADDED + side * (ORDER * NQ) + b] for b in range(NQ)]
+        terms = lines(vals, SCALED, 1)
+        terms = [terms[b] * owners + faces[side * NQ + b] * vals[b] for b in range(NQ)]
+        wait_face(step, c, side)
+        for b in range(NQ):
+            terms[b] = terms[b] + (sent[step, c, side, b] + got[step, c, side, b])
+        terms[0], terms[ORDER] = join_rows(terms[0], terms[ORDER])
+        for b in range(NQ):
+            update(c * PADDED, side * (ORDER * NQ) + b, terms[b], keep, gain)
 
     def prepare_edges(c):
         for b in range(NQ):
             vals = [direction[c * PADDED + a * NQ + b] for a in range(1, ORDER)]
             edges[c * 2 * NQ + b], edges[c * 2 * NQ + NQ + b] = edge_lines([None] + vals + [None])
 
-    def send_edges(step, c):
-        base = c * PADDED
-        own, across = float(SCALED[0, 0]), float(SCALED[0, ORDER])
-        for side in range(2):
-            node = edge_rows[side] * NQ
-            other = edge_rows[1 - side] * NQ
-            vals = [direction[base + node + b] for b in range(NQ)]
-            terms = lines(vals, SCALED, 1)
-            for b in range(NQ):
-                first = edges[c * 2 * NQ + side * NQ + b] + direction[base + other + b] * across
-                terms[b] = terms[b] + first + vals[b] * (coeff[node + b] + own)
-            terms[0], terms[ORDER] = join_rows(terms[0], terms[ORDER])
-            for b in range(NQ):
-                sent[step, c, side, b] = terms[b]
-        start_faces(step, c)
+    def send_face(step, c, side):
+        other = c * PADDED + (1 - side) * (ORDER * NQ)
+        for b in range(NQ):
+            across = direction[other + b] * float(SCALED[0, ORDER])
+            sent[step, c, side, b] = edges[(c * 2 + side) * NQ + b] + across
+        start_face(step, c, side)
 
     def interior(step, c):
         base = c * PADDED
@@ -497,24 +517,32 @@
         lax.fori_loop(1, ORDER, along_second, 0, unroll=UNROLL)
         prepare_edges(c)
 
+    def advance(step, c):
+        send_face(step + 1, c, outer)
+        interior(step + 1, c)
+        finish_face(step + 1, c, outer)
+
     def sweep(q, _):
         step, c = q // COMPS, q % COMPS
-        finish_faces(step, c)
-        send_edges(step + 1, c)
-        interior(step + 1, c)
+        finish_face(step, c, inner)
+        advance(step, c)
+        send_face(step + 2, c, inner)
         return 0
 
-    begin(0)
-    finish_faces(0, 0)
     for c in range(COMPS):
-        send_edges(1, c)
-        interior(1, c)
-        if c + 1 < COMPS:
-            begin(c + 1)
-    lax.fori_loop(COMPS, (ITERS - 1) * COMPS, sweep, 0)
+        begin(c)
+        if c == 0:
+            finish_rhs(c)
+        send_face(1, c, inner)
+        advance(0, c)
+        send_face(2, c, inner)
+    lax.fori_loop(COMPS, (ITERS - 2) * COMPS, sweep, 0)
+    for c in range(COMPS):
+        finish_face(ITERS - 2, c, inner)
+        advance(ITERS - 2, c)
     saves = []
     for c in range(COMPS):
-        finish_faces(ITERS - 1, c)
+        finish_face(ITERS - 1, c, inner)
         part = pl.ds(c * PADDED, NODES)
         saves.append(pltpu.make_async_copy(out.at[part], result.at[part], out_sem.at[c]))
         saves[-1].start()
@@ -560,6 +588,7 @@
             pltpu.VMEM((NODES, 1, 32), jnp.float32),
             pltpu.VMEM((PADDED, 128), jnp.float32),
             pltpu.VMEM((COMPS * 2 * NQ,) + tile, jnp.float32),
+            pltpu.VMEM((2 * NQ,) + tile, jnp.float32),
             pltpu.VMEM((COMPS * PADDED * 8, 128), jnp.float32),
             pltpu.VMEM((COMPS * OWNERS * CHUNK, 128), jnp.float32),
             pltpu.VMEM((COMPS * OWNERS * CHUNK, 128), jnp.float32),

time: 58.9 us -> 60.4 us (1.025)
  the two profiles are of different devices: /device:TPU:96 before, /device:TPU:3 now
where the time goes in v4:
time: 60.4 us; the launch traced here: 60.3 us
  Pallas kernels  60.3 us (100%)
    pallas_call x1, Pallas kernels, run_step(): pl.pallas_call(step_kernel, out_shape=jax.ShapeDtypeStruct((COMPS * PADDE...  56.2 us
    pallas_call x1, Pallas kernels, unpack_output(): pl.pallas_call(unpack_kernel, out_shape=jax.ShapeDtypeStruct(shape, jnp.f...  4.01 us

profile of v4, /device:TPU:3, one launch (start us, length us, event | category | flops | bytes accessed | tf_op | source)
XLA Modules:
  0.0 60.3 jit_solution(930564892544090373)
XLA Ops:
  0.0 56.2 %step.1.tiles_in = f32[384,8,128]{2,1,0:T(8,128)} custom-call(f32[363,8,128]{2,1,0:T(8,128)} %bitcast.7, bf16[512,512]{1,0:T(8,128)(2,1)} %constant.4.clone.high_in, bf16[512,512]{1,0:T(8,128)(2,1)} %constant.5.clone.low_in, f32[121,1,32]{2,1,0:T(1,128)} %bitcast.8), custom_call_target="tpu_custom_call" | custom-call | tf_op jit(solution)/shard_map/step/pallas_call | solution.py:578
  56.3 4.0 %unpack.1 = f32[11616,32]{1,0:T(8,128)} custom-call(f32[384,8,128]{2,1,0:T(8,128)} %step.1.tiles_in), custom_call_target="tpu_custom_call" | custom-call | tf_op jit(solution)/shard_map/unpack/pallas_call | solution.py:648

commit v5 on v3

--- a/solution.py
+++ b/solution.py
@@ -195,7 +195,7 @@
     load_high = pltpu.make_async_copy(high_in, high, load_sem.at[3])
     load_low = pltpu.make_async_copy(low_in, low, load_sem.at[4])
     load_pen = pltpu.make_async_copy(pen_in, pen_rows, load_sem.at[5])
-    for copy in [loads[0], loads[1], load_high, load_low, loads[2], load_pen]:
+    for copy in [loads[0], loads[1], loads[2], load_high, load_low, load_pen]:
         copy.start()
 
     def chunk(c, owner):
@@ -340,17 +340,17 @@
 
     loads[0].wait()
     loads[1].wait()
-    advect(0)
     advect(1)
     peers = OWNERS - 1 + has[0].astype(jnp.int32) + has[1].astype(jnp.int32)
     pl.semaphore_wait(barrier, peers)
     send_forcing_faces(1)
+    loads[2].wait()
+    advect(2)
+    send_forcing_faces(2)
+    advect(0)
     load_high.wait()
     load_low.wait()
     transform(0)
-    loads[2].wait()
-    advect(2)
-    send_forcing_faces(2)
 
     load_pen.wait()
     for node in range(NODES):
@@ -366,9 +366,6 @@
         def _():
             pen_copy(side).start()
 
-    add_forcing_faces(1)
-    transform(1)
-
     block = lax.broadcasted_iota(jnp.int32, (8, 128), 1) // 32
     row = mode * 32 + block * 8 + lax.broadcasted_iota(jnp.int32, (8, 128), 0)
     wave = (row % MODES).astype(jnp.float32)
@@ -381,6 +378,8 @@
             coeff[a * NQ + b] = value
             inverse[a * NQ + b] = value + (diag[a] + diag[b])
 
+    add_forcing_faces(1)
+    transform(1)
     add_forcing_faces(2)
     transform(2)
 

time: 58.9 us -> 58.6 us (level)
  no operation moved by 1% of the time
where the time goes in v5:
time: 58.6 us; the launch traced here: 58.4 us
  Pallas kernels  58.4 us (100%)
    pallas_call x1, Pallas kernels, run_step(): pl.pallas_call(step_kernel, out_shape=jax.ShapeDtypeStruct((COMPS * PADDE...  54.4 us
    pallas_call x1, Pallas kernels, unpack_output(): pl.pallas_call(unpack_kernel, out_shape=jax.ShapeDtypeStruct(shape, jnp.f...  4.01 us

profile of v5, /device:TPU:96, one launch (start us, length us, event | category | flops | bytes accessed | tf_op | source)
XLA Modules:
  0.0 58.4 jit_solution(15988673391141523286)
XLA Ops:
  0.0 54.4 %step.1.tiles_in = f32[384,8,128]{2,1,0:T(8,128)} custom-call(f32[363,8,128]{2,1,0:T(8,128)} %bitcast.7, bf16[512,512]{1,0:T(8,128)(2,1)} %constant.4.clone.high_in, bf16[512,512]{1,0:T(8,128)(2,1)} %constant.5.clone.low_in, f32[121,1,32]{2,1,0:T(1,128)} %bitcast.8), custom_call_target="tpu_custom_call" | custom-call | tf_op jit(solution)/shard_map/step/pallas_call | solution.py:549
  54.4 4.0 %unpack.1 = f32[11616,32]{1,0:T(8,128)} custom-call(f32[384,8,128]{2,1,0:T(8,128)} %step.1.tiles_in), custom_call_target="tpu_custom_call" | custom-call | tf_op jit(solution)/shard_map/unpack/pallas_call | solution.py:618

commit v6 on v5

--- a/solution.py
+++ b/solution.py
@@ -237,19 +237,15 @@
             device_id_type=MESH,
         )
 
-    def start_faces(step, c):
-        for side in range(2):
-
-            @pl.when(has[side])
-            def _():
-                face_copy(step, c, side).start()
-
-    def wait_faces(step, c):
-        for side in range(2):
-
-            @pl.when(has[side])
-            def _():
-                face_copy(step, c, 1 - side).wait_recv()
+    def start_face(step, c, side):
+        @pl.when(has[side])
+        def _():
+            face_copy(step, c, side).start()
+
+    def wait_face(step, c, side):
+        @pl.when(has[side])
+        def _():
+            face_copy(step, c, 1 - side).wait_recv()
 
     for side in range(2):
 
@@ -299,11 +295,11 @@
         for side in range(2):
             for b in range(NQ):
                 sent[0, c, side, b] = forcing[node_rows(c, edge_rows[side] * NQ + b), :]
-        start_faces(0, c)
+            start_face(0, c, side)
 
     def add_forcing_faces(c):
-        wait_faces(0, c)
         for side in range(2):
+            wait_face(0, c, side)
             for b in range(NQ):
                 forcing[node_rows(c, edge_rows[side] * NQ + b), :] += got[0, c, side, b]
 
@@ -429,7 +425,7 @@
                     store(res, node, zero)
                     direction[node] = zero
                     out[node] = zero
-            start_faces(0, c)
+                start_face(0, c, side)
             nodes = range(NQ, NODES - NQ)
         for i in nodes:
             value = inverse[i] * load(res, c * PADDED + i) * CHEBYSHEV[0][1]
@@ -445,9 +441,9 @@
         out[base + node] += value
 
     def finish_faces(step, c):
-        wait_faces(step, c)
         keep, gain = coefficients(step)
         for side in range(2):
+            wait_face(step, c, side)
             for b in range(NQ):
                 change = sent[step, c, side, b] + got[step, c, side, b]
                 update(c * PADDED, edge_rows[side] * NQ + b, change, keep, gain)
@@ -471,7 +467,7 @@
             terms[0], terms[ORDER] = join_rows(terms[0], terms[ORDER])
             for b in range(NQ):
                 sent[step, c, side, b] = terms[b]
-        start_faces(step, c)
+            start_face(step, c, side)
 
     def interior(step, c):
         base = c * PADDED

time: 58.6 us -> 58.8 us (level)
  no operation moved by 1% of the time
where the time goes in v6:
time: 58.8 us; the launch traced here: 58.7 us
  Pallas kernels  58.7 us (100%)
    pallas_call x1, Pallas kernels, run_step(): pl.pallas_call(step_kernel, out_shape=jax.ShapeDtypeStruct((COMPS * PADDE...  54.7 us
    pallas_call x1, Pallas kernels, unpack_output(): pl.pallas_call(unpack_kernel, out_shape=jax.ShapeDtypeStruct(shape, jnp.f...  4.01 us

profile of v6, /device:TPU:96, one launch (start us, length us, event | category | flops | bytes accessed | tf_op | source)
XLA Modules:
  0.0 58.7 jit_solution(4592946998257321299)
XLA Ops:
  0.0 54.7 %step.1.tiles_in = f32[384,8,128]{2,1,0:T(8,128)} custom-call(f32[363,8,128]{2,1,0:T(8,128)} %bitcast.7, bf16[512,512]{1,0:T(8,128)(2,1)} %constant.4.clone.high_in, bf16[512,512]{1,0:T(8,128)(2,1)} %constant.5.clone.low_in, f32[121,1,32]{2,1,0:T(1,128)} %bitcast.8), custom_call_target="tpu_custom_call" | custom-call | tf_op jit(solution)/shard_map/step/pallas_call | solution.py:545
  54.7 4.0 %unpack.1 = f32[11616,32]{1,0:T(8,128)} custom-call(f32[384,8,128]{2,1,0:T(8,128)} %step.1.tiles_in), custom_call_target="tpu_custom_call" | custom-call | tf_op jit(solution)/shard_map/unpack/pallas_call | solution.py:614
